TPU v7x, 256 devices: a whole 4x4x8 slice. The times are simulated.
256 devices in a mesh: req: 8 (over x, y_lo), sp: 32 (over y_hi, z, core).
Axes of the slice: x: 4, y: 4 (y_hi: 2, y_lo: 2; y = y_hi * 2 + y_lo), z: 8, core: 2. Of those that a mesh axis runs over, the one named last changes fastest.
Arguments:
- hidden_feats: bfloat16 [65536, 5120], P('req', 'sp'), parts along dimension 0, may hold values from -6 to 6
- mod_shift: float32 [40960], P(('req', 'sp')), parts along dimension 0, may hold values from -3 to 3
- mod_scale: float32 [40960], P(('req', 'sp')), parts along dimension 0, may hold values from -3 to 3
- head_w: bfloat16 [5120, 64], P('sp'), may hold values from -0.078125 to 0.078125
- head_b: float32 [64], replicated, may hold values from -3 to 3
- latent_mean: float32 [16], replicated, may hold values from -3 to 3
- latent_std: float32 [16], replicated, may hold values from 0.5 to 3
- conv_in_w: bfloat16 [3, 3, 3, 16, 384], replicated, may hold values from -0.3125 to 0.3125
- conv_in_b: float32 [384], replicated, may hold values from -3 to 3
- up_w: bfloat16 [3, 3, 384, 192], replicated, may hold values from -0.109375 to 0.109375
- up_b: float32 [192], replicated, may hold values from -3 to 3
Outputs:
- decoded: bfloat16 [64, 64, 256, 192], P('req', None, 'sp'), parts along dimension 0
There are 8 independent parts, one for each index of `req`. A program takes and returns all parts, laid end to end along the dimension named above; an argument that names none is the same for every part. Nothing has to cross between parts.
All inputs are finite; a program needn't handle non-finite values.
Results may differ from a plain program's by a relative error of at most 0.0062.
Values may be sent and summed in bfloat16 or wider, within the bound.
A program may use at most 64 MiB of HBM per device.

v0:
```python
import jax
import jax.numpy as jnp
from jax import lax
from jax.sharding import PartitionSpec as P

D = 5120
FR = 8
HP = 16
WPD = 2


def padded_2(block, sides, width):
    for axis, dim in sides:
        count = lax.axis_size(axis)
        forward = [(i, i + 1) for i in range(count - 1)]
        backward = [(target, source) for source, target in forward]
        low = lax.ppermute(
            lax.slice_in_dim(block, block.shape[dim] - width, None, axis=dim), axis, forward
        )
        high = lax.ppermute(lax.slice_in_dim(block, 0, width, axis=dim), axis, backward)
        block = jnp.concatenate([low, block, high], axis=dim)
    return block


def first_conv(padded_cols, conv_in_w, conv_in_b):
    padded = jnp.pad(padded_cols, ((2, 0), (1, 1), (0, 0), (0, 0)))
    conved = lax.conv_general_dilated(
        padded[None],
        conv_in_w,
        (1, 1, 1),
        "VALID",
        dimension_numbers=("NDHWC", "DHWIO", "NDHWC"),
        preferred_element_type=jnp.float32,
    )[0]
    return (conved + conv_in_b).astype(jnp.bfloat16)


def second_conv(upsampled_cols, up_w, up_b):
    padded = jnp.pad(upsampled_cols, ((0, 0), (1, 1), (0, 0), (0, 0)))
    upconv = lax.conv_general_dilated(
        padded,
        up_w,
        (1, 1),
        "VALID",
        dimension_numbers=("NHWC", "HWIO", "NHWC"),
        preferred_element_type=jnp.float32,
    )
    return (upconv + up_b).astype(jnp.bfloat16)


def shards(
    hidden_feats,
    mod_shift,
    mod_scale,
    head_w,
    head_b,
    latent_mean,
    latent_std,
    conv_in_w,
    conv_in_b,
    up_w,
    up_b,
):
    feats = hidden_feats.astype(jnp.float32)
    totals = lax.psum((jnp.sum(feats, axis=1), jnp.sum(feats * feats, axis=1)), "sp")
    mean = totals[0] / D
    var = totals[1] / D - mean * mean
    normed = (
        (feats - mean[:, None]) * lax.rsqrt(var + 1e-06)[:, None] * (1.0 + mod_scale) + mod_shift
    ).astype(jnp.bfloat16)
    groups = lax.axis_size("sp")
    channels = latent_std.shape[0]
    patch_width = head_w.shape[1]
    token_count = normed.shape[0]
    local_rows = token_count // groups
    summed = lax.psum_scatter(
        jnp.dot(normed, head_w, preferred_element_type=jnp.float32),
        "sp",
        scatter_dimension=0,
        tiled=True,
    )
    std_row = jnp.tile(latent_std, patch_width // channels)
    mean_row = jnp.tile(latent_mean, patch_width // channels)
    lat_tokens = ((summed + head_b) * std_row + mean_row).astype(jnp.bfloat16)
    pieces = lat_tokens.reshape(local_rows // (WPD * groups), groups, WPD * patch_width)
    strip = lax.all_to_all(pieces, "sp", split_axis=1, concat_axis=0, tiled=True)
    strip = strip.reshape(FR * HP, WPD * patch_width)
    latent = (
        strip.reshape(FR, HP, WPD, 2, 2, channels)
        .transpose(0, 1, 3, 2, 4, 5)
        .reshape(FR, 2 * HP, 2 * WPD, channels)
    )
    latent_wide = padded_2(latent, (("sp", 2),), 1)
    hidden = first_conv(latent_wide, conv_in_w, conv_in_b)
    upsampled = jnp.repeat(jnp.repeat(hidden, 2, axis=1), 2, axis=2)
    upsampled_wide = padded_2(upsampled, (("sp", 2),), 1)
    return second_conv(upsampled_wide, up_w, up_b)


def solution(mesh):
    placed = (
        P("req", "sp"),
        P(("req", "sp")),
        P(("req", "sp")),
        P("sp", None),
        P(),
        P(),
        P(),
        P(),
        P(),
        P(),
        P(),
    )
    return jax.shard_map(
        shards, mesh=mesh, in_specs=placed, out_specs=P("req", None, "sp", None), check_vma=False
    )
```

profile of v0, /device:TPU:1, one launch (start us, length us, event | category | flops | bytes accessed | tf_op | source)
XLA Modules:
  0.0 427.4 jit_solution(11452202365907794205)
XLA Ops:
  6.5 0.0 copy-start
  6.5 0.0 copy-start.2
  6.5 0.0 copy-start.7
  6.5 0.0 copy-start.8
  6.5 0.0 all-reduce.4.cloned.1.call-start
  6.6 3.2 convert_reduce_fusion
  9.8 0.0 all-reduce.4.cloned.1.call-update
  9.9 0.0 reduce-scatter.2.cloned.1.call-start
  9.9 0.0 copy-done.2
  9.9 236.1 %all-reduce.4.cloned.1.call-done = (f32[8192]{0:T(1024)}, f32[8192]{0:T(1024)}) async-done(((f32[8192]{0:T(1024)}, f32[8192]{0:T(1024)}), (f32[8192]{0:T(1024)}, f32[8192]{0:T(1024)})) %all-reduce.4.cloned.1.call-update) | async-done | bytes 65552 | tf_op jit(solution)/shard_map/psum | solution.py:65
  246.1 0.8 broadcast_multiply_fusion
  246.8 0.0 copy-done.7
  246.9 0.0 copy-done.8
  246.9 0.0 copy-start.4
  246.9 0.0 copy-start.5
  246.9 0.0 copy-start.3
  246.9 4.3 %fusion.11 = f32[8192,64]{0,1:T(8,128)} fusion(bf16[160,64]{0,1:T(8,128)(2,1)S(1)} %copy-done.7, bf16[8192,160]{0,1:T(8,128)(2,1)} %param.11, f32[160]{0:T(256)S(1)} %copy-done.8, f32[160]{0:T(256)S(1)} %broadcast_add_fusion, f32[8192]{0:T(1024)S(1)} %get-tuple-element.14, f32[8192]{0:T(1024)S(1)} %get-tuple-element.13), kind=kOutput, calls=%fused_computation.15 | convolution fusion | flops 175636480 | bytes 4805888 | tf_op jit(solution)/shard_map/dot_general | solution.py:77
  251.2 0.0 copy-start.6
  251.3 0.0 reduce-scatter.2.cloned.1.call-update
  251.3 0.0 copy-done.4
  251.3 0.1 add.70
  251.4 0.0 copy-done.5
  251.4 0.1 mul.38
  251.5 111.0 %reduce-scatter.2.cloned.1.call-done = f32[256,64]{0,1:T(8,128)} async-done(((f32[8192,64]{0,1:T(8,128)}), f32[256,64]{0,1:T(8,128)}) %reduce-scatter.2.cloned.1.call-update) | async-done | bytes 65552 | tf_op jit(solution)/shard_map/reduce_scatter | solution.py:76
  362.5 0.0 copy-done.3
  362.5 0.9 add_convert_fusion.1
  363.4 0.1 copy.26
  363.5 0.1 reshape.24
  363.7 20.8 %all_to_all.15 = bf16[4,32,128]{2,0,1:T(4,128)(2,1)S(1)} all-to-all(bf16[4,32,128]{2,0,1:T(4,128)(2,1)S(1)} %copy.27), channel_id=1, replica_groups=mesh['req'=8,'sp'=32] {'sp'}, dimensions={1} | all-to-all | bytes 65536 | tf_op jit(solution)/shard_map/all_to_all | solution.py:86
  384.5 0.2 reshape_reshape.3
  384.7 0.3 copy.28
  385.0 3.0 collective-permute-start
  388.1 1.9 collective-permute-start.1
  390.0 0.0 collective-permute-done
  390.0 3.6 collective-permute-done.1
  393.6 0.3 fusion.30
  394.0 0.0 copy-done.6
  394.0 0.0 copy-start.1
  394.0 3.9 fusion.25
  397.9 0.0 copy-done.1
  397.9 0.4 fusion.24
  398.3 0.7 copy.31
  399.1 0.2 broadcast_in_dim.7
  399.3 0.0 copy-start.9
  399.3 0.3 broadcast_in_dim.8
  399.6 0.1 fusion.34
  399.7 1.9 collective-permute-start.2
  401.6 2.6 collective-permute-start.3
  404.2 2.1 collective-permute-done.2
  406.3 4.4 %collective-permute-done.3 = bf16[8,64,1,384]{3,0,2,1:T(8,128)(2,1)S(1)} collective-permute-done((bf16[8,64,1,384]{3,0,2,1:T(8,128)(2,1)S(1)}, bf16[8,64,1,384]{3,0,2,1:T(8,128)(2,1)S(1)}, u32[]{:S(2)}, u32[]{:S(2)}) %collective-permute-start.3) | collective-permute-done | bytes 393248 | tf_op jit(solution)/shard_map/ppermute | solution.py:20
  410.7 0.0 copy-done
  410.7 0.0 copy-done.9
  410.7 8.1 %add_convert_fusion = bf16[8,64,8,192]{3,0,2,1:T(8,128)(2,1)S(1)} fusion(f32[192]{0:T(256)S(1)} %copy-done.9, bf16[3,3,384,192]{2,3,1,0:T(8,128)(2,1)S(1)} %copy-done, bf16[8,64,1,384]{3,0,2,1:T(8,128)(2,1)S(1)} %collective-permute-done.3, bf16[8,64,8,384]{3,0,2,1:T(8,128)(2,1)S(1)} %bitcast.20, bf16[8,64,1,384]{3,0,2,1:T(8,128)(2,1)S(1)} %collective-permute-done.2), kind=kOutput, calls=%fused_computation.8 | convolution fusion | flops 5392564224 | bytes 6832896 | tf_op jit(solution)/shard_map/conv_general_dilated | solution.py:40
  418.9 1.7 copy.32
  (5 shorter events, 0.0 us)
Async XLA Ops:
  6.5 404.2 %copy-start = (bf16[3,3,384,192]{2,3,1,0:T(8,128)(2,1)S(1)}, bf16[3,3,384,192]{2,3,1,0:T(8,128)(2,1)}, u32[]{:S(2)}) copy-start(bf16[3,3,384,192]{2,3,1,0:T(8,128)(2,1)} %param.20) | copy-start | bytes 3981316
  6.5 3.4 copy-start.2
  6.5 240.3 %copy-start.7 = (bf16[160,64]{0,1:T(8,128)(2,1)S(1)}, bf16[160,64]{0,1:T(8,128)(2,1)}, u32[]{:S(2)}) copy-start(bf16[160,64]{0,1:T(8,128)(2,1)} %param.14) | copy-start | bytes 61444
  6.5 240.3 %copy-start.8 = (f32[160]{0:T(256)S(1)}, f32[160]{0:T(256)}, u32[]{:S(2)}) copy-start(f32[160]{0:T(256)} %param.12) | copy-start | bytes 1924
  6.5 239.5 %all-reduce.4.cloned.1.call-start = ((), (), s32[]{:S(2)}) async-start(), calls=%async_computation.3 | async-start | bytes 131072 | tf_op jit(solution)/shard_map/psum | solution.py:65
  9.9 352.6 %reduce-scatter.2.cloned.1.call-start = ((), (), s32[]{:S(2)}) async-start(), calls=%async_computation.2 | async-start | bytes 2162688 | tf_op jit(solution)/shard_map/reduce_scatter | solution.py:76
  246.9 4.4 %copy-start.4 = (f32[16]{0:T(128)S(1)}, f32[16]{0:T(128)}, u32[]{:S(2)}) copy-start(f32[16]{0:T(128)} %param.16) | copy-start | bytes 196
  246.9 4.5 %copy-start.5 = (f32[16]{0:T(128)S(1)}, f32[16]{0:T(128)}, u32[]{:S(2)}) copy-start(f32[16]{0:T(128)} %param.17) | copy-start | bytes 196
  246.9 115.6 %copy-start.3 = (f32[64]{0:T(128)S(1)}, f32[64]{0:T(128)}, u32[]{:S(2)}) copy-start(f32[64]{0:T(128)} %param.15) | copy-start | bytes 772
  251.2 142.7 %copy-start.6 = (bf16[3,3,3,16,384]{4,3,2,1,0:T(8,128)(2,1)S(1)}, bf16[3,3,3,16,384]{4,3,2,1,0:T(8,128)(2,1)}, u32[]{:S(2)}) copy-start(bf16[3,3,3,16,384]{4,3,2,1,0:T(8,128)(2,1)} %param.18) | copy-start | bytes 995332
  385.0 5.0 %collective-permute-start = (bf16[8,32,1,16]{3,0,2,1:T(8,128)(2,1)S(1)}, bf16[8,32,1,16]{3,0,2,1:T(8,128)(2,1)S(1)}, u32[]{:S(2)}, u32[]{:S(2)}) collective-permute-start(bf16[8,32,1,16]{3,0,2,1:T(8,128)(2,1)S(1)} %get-tuple-element.11), channel_id=1, source_target_pairs={{0,1},{1,2},{2,3},{3,4},{4,5},{5,6},{6,7},{7,8},{8,9},{9,10},{10,1... | collective-permute-start | bytes 24584 | tf_op jit(solution)/shard_map/ppermute | solution.py:17
  388.1 5.6 %collective-permute-start.1 = (bf16[8,32,1,16]{3,0,2,1:T(8,128)(2,1)S(1)}, bf16[8,32,1,16]{3,0,2,1:T(8,128)(2,1)S(1)}, u32[]{:S(2)}, u32[]{:S(2)}) collective-permute-start(bf16[8,32,1,16]{3,0,2,1:T(8,128)(2,1)S(1)} %get-tuple-element.12), channel_id=1, source_target_pairs={{1,0},{2,1},{3,2},{4,3},{5,4},{6,5},{7,6},{8,7},{9,8},{10,9},{11,1... | collective-permute-start | bytes 24584 | tf_op jit(solution)/shard_map/ppermute | solution.py:20
  394.0 3.9 copy-start.1
  399.3 11.5 %copy-start.9 = (f32[192]{0:T(256)S(1)}, f32[192]{0:T(256)}, u32[]{:S(2)}) copy-start(f32[192]{0:T(256)} %param.21) | copy-start | bytes 2308
  399.7 6.6 %collective-permute-start.2 = (bf16[8,64,1,384]{3,0,2,1:T(8,128)(2,1)S(1)}, bf16[8,64,1,384]{3,0,2,1:T(8,128)(2,1)S(1)}, u32[]{:S(2)}, u32[]{:S(2)}) collective-permute-start(bf16[8,64,1,384]{3,0,2,1:T(8,128)(2,1)S(1)} %get-tuple-element.9), channel_id=1, source_target_pairs={{0,1},{1,2},{2,3},{3,4},{4,5},{5,6},{6,7},{7,8},{8,9},{9,10},{10,1... | collective-permute-start | bytes 1179656 | tf_op jit(solution)/shard_map/ppermute | solution.py:17
  401.6 9.1 %collective-permute-start.3 = (bf16[8,64,1,384]{3,0,2,1:T(8,128)(2,1)S(1)}, bf16[8,64,1,384]{3,0,2,1:T(8,128)(2,1)S(1)}, u32[]{:S(2)}, u32[]{:S(2)}) collective-permute-start(bf16[8,64,1,384]{3,0,2,1:T(8,128)(2,1)S(1)} %get-tuple-element.10), channel_id=1, source_target_pairs={{1,0},{2,1},{3,2},{4,3},{5,4},{6,5},{7,6},{8,7},{9,8},{10,9},{11,1... | collective-permute-start | bytes 1179656 | tf_op jit(solution)/shard_map/ppermute | solution.py:20
Sparse Core Ops, SparseCore 0:
  10.1 235.9 all-reduce.3
  251.4 111.0 reduce-scatter.1
where the time goes:
time: 431 us; the launch traced here: 427 us
  waiting for transfers between devices  357 us (83%)
  blocking collectives  20.8 us (5%)
  matrix products  16.4 us (4%)
  between operations  13.7 us (3%)
  starting transfers between devices  9.54 us (2%)
  other arithmetic  5.7 us (1%)
    psum x1, waiting for transfers between devices, shards(): lax.psum((jnp.sum(feats, axis=1), jnp.sum(feats * feats, axis=1)), 'sp')  236 us
    reduce_scatter x1, waiting for transfers between devices, shards(): lax.psum_scatter(jnp.dot(normed, head_w, preferred_element_type=jnp.float...  111 us
    all_to_all x1, blocking collectives, shards(): lax.all_to_all(pieces, 'sp', split_axis=1, concat_axis=0, tiled=True)  20.8 us
  transfers between devices with their start and end apart: 6, of which 5 were waited for; matrix products, arithmetic and copies ran while one was open for 0% of the time, Pallas kernels for 0%

commit v1 on v0

v1 whole, which is shorter than its diff:
```python
import functools

import jax
import jax.numpy as jnp
from jax import lax
from jax.experimental import pallas as pl
from jax.experimental.pallas import tpu as pltpu
from jax.sharding import PartitionSpec as P

F32 = jnp.float32
BF16 = jnp.bfloat16
MESH = pl.DeviceIdType.MESH

FEATS = 5120
LOCAL = 160
FRAMES = 8
CHIPS = 16
GROUP = 32
OFFSETS = [(dy, dz) for dz in (4, 3, 5, 2, 6, 1, 7) for dy in (1, 0)] + [(1, 0), (0, 0)]


def lanes(shape):
    return lax.broadcasted_iota(jnp.int32, shape, len(shape) - 1)


def rows(shape):
    return lax.broadcasted_iota(jnp.int32, shape, len(shape) - 2)


def to_column(row):
    width = row.shape[1]
    square = (width, width)
    return jnp.sum(jnp.where(rows(square) == lanes(square), row, 0.0), axis=1, keepdims=True)


def tile16(row):
    wide = jnp.concatenate([row, jnp.zeros((1, 112), F32)], axis=1)
    for step in (16, 32, 64):
        wide = wide + pltpu.roll(wide, step, 1)
    return wide


def head_kernel(
    x_hbm, shift_ref, scale_ref, head_w_ref, head_b_ref, lat_mean_ref, lat_std_ref,
    out_ref,
    x_buf, partial, sums, squares, own_stat, peer_stat, give, got, kept, parcel, arrived,
    stat_out, stat_in, strip,
    x_sem, stat_sem, core_send, core_recv, send_sem, recv_sem, ssend_sem, srecv_sem, halo_sem,
):
    me = lax.axis_index("sp")
    req = lax.axis_index("req")
    core = lax.rem(me, 2)
    chip = me // 2
    y, z = chip // 8, lax.rem(chip, 8)

    def chip_at(offset):
        dy, dz = offset
        return lax.rem(y + dy, 2) * 8 + lax.rem(z + dz, 8)

    def device(sp):
        return (req, sp)

    partner = chip * 2 + (1 - core)
    left, right = lax.rem(me + GROUP - 1, GROUP), lax.rem(me + 1, GROUP)
    other = jnp.where(core == 0, left, right)

    x_copies = []
    for f in range(FRAMES):
        copy = pltpu.make_async_copy(x_hbm.at[pl.ds(f * 1024, 1024)], x_buf.at[f], x_sem.at[f])
        copy.start()
        x_copies.append(copy)

    barrier = pltpu.get_barrier_semaphore()
    for offset in OFFSETS[:-1]:
        pl.semaphore_signal(barrier, inc=1, device_id=device(chip_at(offset) * 2 + core), device_id_type=MESH)
    pl.semaphore_signal(barrier, inc=1, device_id=device(partner), device_id_type=MESH)
    pl.semaphore_signal(barrier, inc=1, device_id=device(other), device_id_type=MESH)

    scale = to_column(scale_ref[...].reshape(1, LOCAL))
    shift = to_column(shift_ref[...].reshape(1, LOCAL))
    head = head_w_ref[...].astype(F32)
    folded = (1.0 + scale) * head
    column_sum = jnp.sum(folded, axis=0, keepdims=True)
    shifted = jnp.sum(shift * head, axis=0, keepdims=True)
    centred = folded - column_sum * (1.0 / LOCAL)
    high = centred.astype(BF16)
    low = (centred - high.astype(F32)).astype(BF16)
    high = jnp.concatenate([high, high], axis=1)
    low = jnp.concatenate([low, low], axis=1)
    ones = jnp.ones((8, LOCAL), BF16)
    diagonal = rows((128, 128)) == lanes((128, 128))

    for f in range(FRAMES):
        x_copies[f].wait()

        def block(i, carry):
            x = x_buf[f, pl.ds(pl.multiple_of(i * 128, 128), 128), :]
            value = jnp.dot(x, high, preferred_element_type=F32) + jnp.dot(x, low, preferred_element_type=F32)
            partial[pl.ds(pl.multiple_of(f * 1024 + i * 128, 128), 128), :] = value
            transposed = (((1,), (1,)), ((), ()))
            total = lax.dot_general(ones, x, transposed, preferred_element_type=F32)
            gram = lax.dot_general(x, x, transposed, preferred_element_type=F32)
            sums[pl.ds(f * 8 + i, 1), :] = total[0:1, :]
            squares[pl.ds(f * 8 + i, 1), :] = jnp.sum(jnp.where(diagonal, gram, 0.0), axis=0, keepdims=True)
            return carry

        lax.fori_loop(0, 8, block, 0, unroll=True)

    lower = lanes((64, 128)) < 64
    turned = jnp.transpose(jnp.concatenate([sums[...], squares[...]], axis=0))
    top, bottom = turned[0:64], turned[64:128]
    own_stat[0:64, :] = jnp.where(lower, top, pltpu.roll(bottom, 64, 1))
    own_stat[64:128, :] = jnp.where(lower, pltpu.roll(top, 64, 1), bottom)
    own_row = jnp.concatenate([column_sum, shifted], axis=1)
    own_stat[128:136, :] = jnp.broadcast_to(own_row, (8, 128))

    pl.semaphore_wait(barrier, 17)

    stat_copy = pltpu.make_async_remote_copy(
        src_ref=own_stat, dst_ref=peer_stat, send_sem=stat_sem.at[0], recv_sem=stat_sem.at[1],
        device_id=device(partner), device_id_type=MESH,
    )
    stat_copy.start()

    def gathered(chip_to, core_to):
        parts = []
        for parity in range(2):
            at = parity * 64 + (chip_to * 2 + core_to) * 2
            even = partial[pl.ds(at, 64, stride=128), :]
            odd = partial[pl.ds(at + 1, 64, stride=128), :]
            parts.append(jnp.where(lower, even, odd))
        return jnp.concatenate(parts, axis=0)

    core_copies = []
    for k, offset in enumerate(OFFSETS):
        give[k] = gathered(chip_at(offset), 1 - core).astype(BF16)
        copy = pltpu.make_async_remote_copy(
            src_ref=give.at[k], dst_ref=got.at[k], send_sem=core_send.at[k], recv_sem=core_recv.at[k],
            device_id=device(partner), device_id_type=MESH,
        )
        copy.start()
        core_copies.append(copy)

    stat_copy.wait()
    own_last, peer_last = own_stat[128:129, :], peer_stat[128:129, :]
    low_row = lanes((1, 128)) < 64
    both = jnp.where(low_row, own_last, pltpu.roll(peer_last, 64, 1))
    shift_row = pltpu.roll(own_last + peer_last, 64, 1)

    copies = []
    for k, offset in enumerate(OFFSETS):
        to = chip_at(offset)
        at = to * 4 + core * 2
        stat_out[k, 0:2, :] = own_stat[pl.ds(at, 2), :]
        stat_out[k, 2:4, :] = peer_stat[pl.ds(at, 2), :]
        stat_out[k, 4:6, :] = own_stat[pl.ds(at + 64, 2), :] + peer_stat[pl.ds(at + 64, 2), :]
        stat_out[k, 6:7, :] = both
        stat_out[k, 7:8, :] = shift_row
        core_copies[k].wait_recv()
        merged = gathered(to, core) + got[k].astype(F32)
        if k == CHIPS - 1:
            kept[...] = merged
            stat_in[k] = stat_out[k]
            continue
        parcel[k] = merged.astype(BF16)
        target = device(to * 2 + core)
        for src, dst, out_sem, in_sem in (
            (stat_out, stat_in, ssend_sem, srecv_sem),
            (parcel, arrived, send_sem, recv_sem),
        ):
            copy = pltpu.make_async_remote_copy(
                src_ref=src.at[k], dst_ref=dst.at[k], send_sem=out_sem.at[k], recv_sem=in_sem.at[k],
                device_id=target, device_id_type=MESH,
            )
            copy.start()
            copies.append(copy)

    for copy in copies:
        copy.wait_recv()
    total = kept[...]
    for k in range(CHIPS - 1):
        total = total + arrived[k].astype(F32)

    stat = stat_in[...]
    summed = jnp.sum(stat, axis=0)
    row_of = rows((128, 128))
    line = lax.rem(row_of, 8)
    mean_even = (summed[0:1] + summed[2:3]) * (1.0 / FEATS)
    mean_odd = (summed[1:2] + summed[3:4]) * (1.0 / FEATS)
    rstd_even = lax.rsqrt(summed[4:5] * (1.0 / FEATS) - mean_even * mean_even + 1e-06)
    rstd_odd = lax.rsqrt(summed[5:6] * (1.0 / FEATS) - mean_odd * mean_odd + 1e-06)
    offcentre = stat.reshape(128, 128) * (1.0 / LOCAL) - jnp.where(lax.rem(row_of, 2) == 0, mean_even, mean_odd)
    offcentre = jnp.where(line < 4, offcentre, 0.0)
    heads = jnp.broadcast_to(stat[:, 6:7, :], (CHIPS, 8, 128)).reshape(128, 128)
    swapped = pltpu.roll(heads, 64, 1)
    left_half = lanes((128, 128)) < 64
    zero = jnp.zeros((128, 128), F32)
    heads = jnp.where(
        line == 0, jnp.where(left_half, heads, zero),
        jnp.where(
            line == 1, jnp.where(left_half, zero, swapped),
            jnp.where(
                line == 2, jnp.where(left_half, swapped, zero),
                jnp.where(line == 3, jnp.where(left_half, zero, heads), zero),
            ),
        ),
    )
    centre = jnp.dot(jnp.transpose(heads), offcentre, precision=lax.Precision.HIGHEST, preferred_element_type=F32)
    bias = summed[7:8] + jnp.concatenate([head_b_ref[...].reshape(1, 64), jnp.zeros((1, 64), F32)], axis=1)
    bias = jnp.where(low_row, bias, pltpu.roll(bias, 64, 1))
    std = tile16(lat_std_ref[...].reshape(1, 16))
    mean = tile16(lat_mean_ref[...].reshape(1, 16))
    patches = (jnp.transpose(total) + centre) * jnp.where(row_of < 64, rstd_even, rstd_odd) + to_column(bias)
    latent = (patches * to_column(std) + to_column(mean)).astype(BF16)
    strip[1] = latent[0:64]
    strip[2] = latent[64:128]
    halos = []
    for src, dst, to in ((1, 3, left), (2, 0, right)):
        copy = pltpu.make_async_remote_copy(
            src_ref=strip.at[src], dst_ref=strip.at[dst], send_sem=halo_sem.at[src], recv_sem=halo_sem.at[dst],
            device_id=device(to), device_id_type=MESH,
        )
        copy.start()
        halos.append(copy)
    out_ref[1] = latent[0:64]
    out_ref[2] = latent[64:128]
    for copy in halos:
        copy.wait_recv()
    out_ref[0] = jnp.where(me == 0, 0.0, strip[0].astype(F32)).astype(BF16)
    out_ref[3] = jnp.where(me == GROUP - 1, 0.0, strip[3].astype(F32)).astype(BF16)
    for copy in core_copies + copies + halos:
        copy.wait_send()


def conv_kernel(
    lat_ref, conv_w_ref, conv_b_ref, up_w_ref, up_b_ref,
    out_hbm,
    taps, weight, phases, wide, stage, ready, out_sem,
):
    me = lax.axis_index("sp")
    lane = lanes((64, 128))
    frame = lax.rem(lane // 8, 8)
    half_row = lax.rem(lane, 8)

    for dx in range(3):
        for j in range(4):
            for kt in range(3):
                at = ((dx * 4 + j) * 3 + kt) * 16
                for q in range(2):
                    inside = 0 <= j - q <= 2
                    tap = conv_w_ref[kt, j - q, dx] if inside else jnp.zeros((16, 384), BF16)
                    weight[at : at + 16, q * 384 : (q + 1) * 384] = tap

    for w in range(4):
        x = lat_ref[w].astype(F32)
        above = jnp.where(lane >= 64, pltpu.roll(x, 64, 1), jnp.where(half_row == 0, 0.0, pltpu.roll(x, 65, 1)))
        below = jnp.where(lane < 64, pltpu.roll(x, 64, 1), jnp.where(half_row == 7, 0.0, pltpu.roll(x, 63, 1)))
        for kt in range(3):
            back = 2 - kt

            def earlier(v):
                if back == 0:
                    return v.astype(BF16)
                return jnp.where(frame >= back, pltpu.roll(v, 8 * back, 1), 0.0).astype(BF16)

            up, here, down = earlier(above), earlier(x), earlier(below)
            for r in range(2):
                for j, (source, q) in enumerate(((up, 1), (here, 0), (here, 1), (down, 0))):
                    at = (((w * 2 + r) * 4 + j) * 3 + kt) * 16
                    taps[at : at + 16, :] = source[q * 32 + r * 16 : q * 32 + r * 16 + 16, :]

    conv_b = conv_b_ref[...].reshape(1, 384)
    conv_b = jnp.concatenate([conv_b, conv_b], axis=1)
    inner = rows((8, 8, 384))
    for m in range(6):
        hidden = lax.dot_general(
            taps[192 * m : 192 * m + 576, :], weight[...], (((0,), (0,)), ((), ())), preferred_element_type=F32
        )
        hidden = hidden + conv_b
        if m == 0:
            hidden = jnp.where(me == 0, 0.0, hidden)
        if m == 5:
            hidden = jnp.where(me == GROUP - 1, 0.0, hidden)
        first, second = hidden[:, 0:384], hidden[:, 384:768]
        before = jnp.where(inner == 0, 0.0, pltpu.roll(second[64:128].reshape(8, 8, 384), 1, 1)).reshape(64, 384)
        after = jnp.where(inner == 7, 0.0, pltpu.roll(first[0:64].reshape(8, 8, 384), 7, 1)).reshape(64, 384)
        at = slice(128 * m, 128 * m + 128)
        wide[at, 0:384] = jnp.concatenate([before, second[0:64]], axis=0).astype(BF16)
        wide[at, 384:768] = first.astype(BF16)
        wide[at, 768:1152] = second.astype(BF16)
        wide[at, 1152:1536] = jnp.concatenate([first[64:128], after], axis=0).astype(BF16)

    def split(first, middle, last):
        return {(0, 0): first, (0, 1): middle + last, (1, 0): first + middle, (1, 1): last}

    def part(i, carry):
        at = pl.multiple_of(i * 32, 32)
        by_column = [
            split(*(up_w_ref[dy, dx, pl.ds(at, 32), :].astype(F32) for dy in range(3))) for dx in range(3)
        ]
        for a in range(2):
            for alpha in range(2):
                combined = split(*(by_column[dx][a, alpha] for dx in range(3)))
                for b in range(2):
                    for beta in range(2):
                        value = combined[b, beta].astype(BF16)
                        row = pl.multiple_of(alpha * 384 + at, 32)
                        phases[a, b, beta, pl.ds(row, 32), 0:192] = value
                        phases[a, b, beta, pl.ds(row, 32), 192:256] = jnp.zeros((32, 64), BF16)
        return carry

    lax.fori_loop(0, 12, part, 0)

    up_b = jnp.concatenate([up_b_ref[...].reshape(1, 192), jnp.zeros((1, 64), F32)], axis=1)
    copies = []
    for p in range(4):
        q, a = p // 2, p % 2
        band = slice((q + a) * 384, (q + a) * 384 + 768)
        for b in range(2):
            value = jnp.dot(wide[b * 128 : b * 128 + 512, band], phases[a, b, 0], preferred_element_type=F32)
            value += jnp.dot(wide[b * 128 + 128 : b * 128 + 640, band], phases[a, b, 1], preferred_element_type=F32)
            value = value + up_b
            for x in range(4):
                for half in range(2):
                    stage[half, pl.ds(2 * x + b, 128, stride=8), :] = value[
                        x * 128 : (x + 1) * 128, half * 128 : (half + 1) * 128
                    ]
        ready[p, :, :, 0:128] = stage[0].reshape(128, 8, 128).astype(BF16)
        ready[p, :, :, 128:192] = stage[1].reshape(128, 8, 128)[:, :, 0:64].astype(BF16)
        for parity in range(2):
            copy = pltpu.make_async_copy(
                ready.at[p, pl.ds(parity * 64, 64)], out_hbm.at[:, parity, p], out_sem.at[p, parity]
            )
            copy.start()
            copies.append(copy)
    for copy in copies:
        copy.wait()


def shards(
    hidden_feats, mod_shift, mod_scale, head_w, head_b, latent_mean, latent_std, conv_in_w, conv_in_b, up_w, up_b
):
    vmem = pl.BlockSpec(memory_space=pltpu.VMEM)
    anywhere = pl.BlockSpec(memory_space=pl.ANY)
    dma = pltpu.SemaphoreType.DMA
    latent = pl.pallas_call(
        head_kernel,
        out_shape=jax.ShapeDtypeStruct((4, 64, 128), BF16),
        in_specs=[anywhere] + [vmem] * 6,
        out_specs=vmem,
        scratch_shapes=[
            pltpu.VMEM((FRAMES, 1024, LOCAL), BF16),
            pltpu.VMEM((8192, 128), F32),
            pltpu.VMEM((64, 128), F32),
            pltpu.VMEM((64, 128), F32),
            pltpu.VMEM((136, 128), F32),
            pltpu.VMEM((136, 128), F32),
            pltpu.VMEM((CHIPS, 128, 128), BF16),
            pltpu.VMEM((CHIPS, 128, 128), BF16),
            pltpu.VMEM((128, 128), F32),
            pltpu.VMEM((CHIPS - 1, 128, 128), BF16),
            pltpu.VMEM((CHIPS - 1, 128, 128), BF16),
            pltpu.VMEM((CHIPS, 8, 128), F32),
            pltpu.VMEM((CHIPS, 8, 128), F32),
            pltpu.VMEM((4, 64, 128), BF16),
            dma((FRAMES,)),
            dma((2,)),
            dma((CHIPS,)),
            dma((CHIPS,)),
            dma((CHIPS,)),
            dma((CHIPS,)),
            dma((CHIPS,)),
            dma((CHIPS,)),
            dma((4,)),
        ],
        compiler_params=pltpu.CompilerParams(
            collective_id=0, has_side_effects=True, vmem_limit_bytes=40 * 1024 * 1024
        ),
        name="head",
    )(hidden_feats, mod_shift, mod_scale, head_w, head_b, latent_mean, latent_std)
    decoded = pl.pallas_call(
        conv_kernel,
        out_shape=jax.ShapeDtypeStruct((64, 2, 4, 8, 192), BF16),
        in_specs=[vmem] * 5,
        out_specs=anywhere,
        scratch_shapes=[
            pltpu.VMEM((8 * 192, 128), BF16),
            pltpu.VMEM((576, 768), BF16),
            pltpu.VMEM((2, 2, 2, 768, 256), BF16),
            pltpu.VMEM((768, 1536), BF16),
            pltpu.VMEM((2, 1024, 128), F32),
            pltpu.VMEM((4, 128, 8, 192), BF16),
            dma((4, 2)),
        ],
        compiler_params=pltpu.CompilerParams(vmem_limit_bytes=40 * 1024 * 1024),
        name="conv",
    )(latent, conv_in_w, conv_in_b, up_w, up_b)
    return decoded.reshape(8, 64, 8, 192)


def solution(mesh):
    placed = (
        P("req", "sp"),
        P(("req", "sp")),
        P(("req", "sp")),
        P("sp", None),
        P(),
        P(),
        P(),
        P(),
        P(),
        P(),
        P(),
    )
    return jax.shard_map(
        shards, mesh=mesh, in_specs=placed, out_specs=P("req", None, "sp", None), check_vma=False
    )
```

time: 431 us -> 50.1 us (0.12)
  waiting for transfers between devices: 357 us -> 0 us
  Pallas kernels: 0 us -> 40.6 us
  blocking collectives: 20.8 us -> 0 us
  matrix products: 16.4 us -> 0 us
  between operations: 13.7 us -> 0.29 us
  starting transfers between devices: 9.54 us -> 0 us
  other arithmetic: 5.7 us -> 0 us
  local copies, waits for them, and re-layouts: 4.03 us -> 8.99 us
    psum x1 -> x0, waiting for transfers between devices: 236 us -> none  [shards(): lax.psum((jnp.sum(feats, axis=1), jnp.sum(feats * feats, axis=1)), 'sp')]
    reduce_scatter x1 -> x0, waiting for transfers between devices: 111 us -> none  [shards(): lax.psum_scatter(jnp.dot(normed, head_w, preferred_element_type=jnp.float...]
    pallas_call x0 -> x2, Pallas kernels: none -> 40.6 us  [the longest x1 33.4 us: shards(): pl.pallas_call(head_kernel, out_shape=jax.ShapeDtypeStruct((4, 64, 128),...]
    all_to_all x1 -> x0, blocking collectives: 20.8 us -> none  [shards(): lax.all_to_all(pieces, 'sp', split_axis=1, concat_axis=0, tiled=True)]
    conv_general_dilated x2 -> x0, matrix products: 12 us -> none  [the longest x1 8.11 us: second_conv(): lax.conv_general_dilated(padded, up_w, (1, 1), 'VALID', dimension_numbers...]
    ppermute x4 -> x0, waiting for transfers between devices: 10.1 us -> none  [the longest x2 8.04 us: padded_2(): lax.ppermute(lax.slice_in_dim(block, 0, width, axis=dim), axis, backward)]
    ppermute x4 -> x0, starting transfers between devices: 9.47 us -> none  [the longest x2 4.94 us: padded_2(): lax.ppermute(lax.slice_in_dim(block, block.shape[dim] - width, None, axis...]
    unnamed x20 -> x25, local copies, waits for them, and re-layouts: 0.05 us -> 8.99 us
  transfers between devices with their start and end apart: 6 -> 0, of which waited for: 5 -> 0; matrix products, arithmetic and copies ran while one was open for 0% -> 0% of each run, Pallas kernels for 0% -> 0%
where the time goes in v1:
time: 50.1 us; the launch traced here: 49.9 us
  Pallas kernels  40.6 us (81%)
  local copies, waits for them, and re-layouts  8.99 us (18%)
    pallas_call x1, Pallas kernels, shards(): pl.pallas_call(head_kernel, out_shape=jax.ShapeDtypeStruct((4, 64, 128),...  33.4 us
    unnamed x25, local copies, waits for them, and re-layouts  8.99 us
    pallas_call x1, Pallas kernels, shards(): pl.pallas_call(conv_kernel, out_shape=jax.ShapeDtypeStruct((64, 2, 4, 8,...  7.23 us

profile of v1, /device:TPU:1, one launch (start us, length us, event | category | flops | bytes accessed | tf_op | source)
XLA Modules:
  0.0 49.9 jit_solution(9486539212466068621)
XLA Ops:
  0.0 0.0 copy-start.10
  0.0 0.0 copy-start.3
  0.0 0.0 copy-start.4
  0.0 0.0 copy-start.6
  0.0 0.0 copy-start.7
  0.0 0.0 copy-start.8
  0.0 5.7 %copy.12.x_hbm = bf16[8192,160]{1,0:T(8,128)(2,1)} copy(bf16[8192,160]{0,1:T(8,128)(2,1)} %param.11) | data formatting | bytes 5242880 | tf_op args[0]
  5.8 0.0 copy-done.10
  5.8 0.1 copy.13.head_w_ref
  5.9 0.0 copy-done.3
  5.9 0.0 copy-done.4
  5.9 0.0 copy-done.6
  5.9 0.0 copy-done.7
  5.9 0.0 copy-done.8
  5.9 0.0 copy-start
  5.9 2.2 %copy-done = bf16[8192,160]{1,0:T(8,128)(2,1)S(1)} copy-done((bf16[8192,160]{1,0:T(8,128)(2,1)S(1)}, bf16[8192,160]{1,0:T(8,128)(2,1)}, u32[]{:S(2)}) %copy-start) | copy-done | bytes 2621464
  8.1 0.0 copy-start.9
  8.1 33.4 %head.1.lat_ref = bf16[4,64,128]{2,1,0:T(8,128)(2,1)S(1)} custom-call(bf16[8192,160]{1,0:T(8,128)(2,1)S(1)} %copy-done, f32[160]{0:T(256)S(1)} %copy-done.3, f32[160]{0:T(256)S(1)} %copy-done.4, bf16[160,64]{1,0:T(8,128)(2,1)S(1)} %copy.13.head_w_ref, f32[64]{0:T(128)S(1)} %copy-done.6, f32[16]{0:T(128)S(1)} %copy-done.7, f32[16]{0:T(128)S(1)} %copy-done.8), custom_call_target="tpu_custom_call" | custom-call | tf_op jit(solution)/shard_map/head/pallas_call | solution.py:346
  41.5 0.0 copy-done.9
  41.5 0.0 copy-start.1
  41.5 0.0 copy-start.2
  41.5 0.0 copy-start.5
  41.5 0.9 %copy.14.up_w_ref = bf16[3,3,384,192]{3,2,1,0:T(8,128)(2,1)S(1)} copy(bf16[3,3,384,192]{2,3,1,0:T(8,128)(2,1)S(1)} %copy-done.9) | data formatting | bytes 2654208 | tf_op args[9]
  42.5 0.0 copy-done.1
  42.5 0.0 copy-done.2
  42.5 0.0 copy-done.5
  42.5 7.2 %conv.1 = bf16[64,2,4,8,192]{4,3,2,1,0:T(8,128)(2,1)} custom-call(bf16[4,64,128]{2,1,0:T(8,128)(2,1)S(1)} %head.1.lat_ref, bf16[3,3,3,16,384]{4,3,2,1,0:T(8,128)(2,1)S(1)} %copy-done.1, f32[384]{0:T(512)S(1)} %copy-done.2, bf16[3,3,384,192]{3,2,1,0:T(8,128)(2,1)S(1)} %copy.14.up_w_ref, f32[192]{0:T(256)S(1)} %copy-done.5), custom_call_target="tpu_custom_call" | custom-call | tf_op jit(solution)/shard_map/conv/pallas_call | solution.py:381
Async XLA Ops:
  0.0 5.8 %copy-start.10 = (bf16[160,64]{0,1:T(8,128)(2,1)S(1)}, bf16[160,64]{0,1:T(8,128)(2,1)}, u32[]{:S(2)}) copy-start(bf16[160,64]{0,1:T(8,128)(2,1)} %param.14) | copy-start | bytes 61444
  0.0 5.9 %copy-start.3 = (f32[160]{0:T(256)S(1)}, f32[160]{0:T(256)}, u32[]{:S(2)}) copy-start(f32[160]{0:T(256)} %shift_ref.1) | copy-start | bytes 1924
  0.0 5.9 %copy-start.4 = (f32[160]{0:T(256)S(1)}, f32[160]{0:T(256)}, u32[]{:S(2)}) copy-start(f32[160]{0:T(256)} %scale_ref.1) | copy-start | bytes 1924
  0.0 5.9 %copy-start.6 = (f32[64]{0:T(128)S(1)}, f32[64]{0:T(128)}, u32[]{:S(2)}) copy-start(f32[64]{0:T(128)} %head_b_ref.1) | copy-start | bytes 772
  0.0 5.9 %copy-start.7 = (f32[16]{0:T(128)S(1)}, f32[16]{0:T(128)}, u32[]{:S(2)}) copy-start(f32[16]{0:T(128)} %lat_mean_ref.1) | copy-start | bytes 196
  0.0 5.9 %copy-start.8 = (f32[16]{0:T(128)S(1)}, f32[16]{0:T(128)}, u32[]{:S(2)}) copy-start(f32[16]{0:T(128)} %lat_std_ref.1) | copy-start | bytes 196
  5.9 2.2 %copy-start = (bf16[8192,160]{1,0:T(8,128)(2,1)S(1)}, bf16[8192,160]{1,0:T(8,128)(2,1)}, u32[]{:S(2)}) copy-start(bf16[8192,160]{1,0:T(8,128)(2,1)} %copy.12.x_hbm) | copy-start | bytes 7864324
  8.1 33.4 %copy-start.9 = (bf16[3,3,384,192]{2,3,1,0:T(8,128)(2,1)S(1)}, bf16[3,3,384,192]{2,3,1,0:T(8,128)(2,1)}, u32[]{:S(2)}) copy-start(bf16[3,3,384,192]{2,3,1,0:T(8,128)(2,1)} %param.20) | copy-start | bytes 3981316
  41.5 1.0 %copy-start.1 = (bf16[3,3,3,16,384]{4,3,2,1,0:T(8,128)(2,1)S(1)}, bf16[3,3,3,16,384]{4,3,2,1,0:T(8,128)(2,1)}, u32[]{:S(2)}) copy-start(bf16[3,3,3,16,384]{4,3,2,1,0:T(8,128)(2,1)} %conv_w_ref.1) | copy-start | bytes 995332
  41.5 1.0 %copy-start.2 = (f32[384]{0:T(512)S(1)}, f32[384]{0:T(512)}, u32[]{:S(2)}) copy-start(f32[384]{0:T(512)} %conv_b_ref.1) | copy-start | bytes 4612
  41.5 1.0 %copy-start.5 = (f32[192]{0:T(256)S(1)}, f32[192]{0:T(256)}, u32[]{:S(2)}) copy-start(f32[192]{0:T(256)} %up_b_ref.1) | copy-start | bytes 2308

commit v2 on v0

v2 whole, which is shorter than its diff:
```python
import jax
import jax.numpy as jnp
from jax import lax
from jax.experimental import pallas as pl
from jax.experimental.pallas import tpu as pltpu
from jax.sharding import PartitionSpec as P

F32 = jnp.float32
BF16 = jnp.bfloat16
MESH = pl.DeviceIdType.MESH

FEATS = 5120
LOCAL = 160
CHUNKS = 4
CHIPS = 16
GROUP = 32
OFFSETS = [(dy, dz) for dz in (4, 3, 5, 2, 6, 1, 7) for dy in (1, 0)] + [(1, 0), (0, 0)]
NT = (((1,), (1,)), ((), ()))


def lanes(shape):
    return lax.broadcasted_iota(jnp.int32, shape, len(shape) - 1)


def rows(shape):
    return lax.broadcasted_iota(jnp.int32, shape, len(shape) - 2)


def square(width):
    return rows((width, width)) == lanes((width, width))


def to_column(row):
    return jnp.sum(jnp.where(square(row.shape[1]), row, 0.0), axis=1, keepdims=True)


def to_row(column):
    return jnp.sum(jnp.where(square(column.shape[0]), column, 0.0), axis=0, keepdims=True)


def tile16(row):
    wide = jnp.concatenate([row, jnp.zeros((1, 112), F32)], axis=1)
    for step in (16, 32, 64):
        wide = wide + pltpu.roll(wide, step, 1)
    return wide[:, 0:64]


def prepare_first(conv_w, first_w):
    for dx in range(3):
        for kt in range(3):
            for j in range(4):
                at = (kt * 4 + j) * 16
                for q in range(2):
                    inside = 0 <= j - q <= 2
                    tap = conv_w[kt, j - q, dx] if inside else jnp.zeros((16, 384), BF16)
                    first_w[dx, at : at + 16, q * 384 : (q + 1) * 384] = tap
        first_w[dx, 192:256, :] = jnp.zeros((64, 768), BF16)


def prepare_second(up_w, second_w):
    def split(first, middle, last):
        return {(0, 0): first, (0, 1): middle + last, (1, 0): first + middle, (1, 1): last}

    def part(i, carry):
        at = pl.ds(pl.multiple_of(i * 16, 16), 16)
        by_column = [split(*(up_w[dy, dx, at, :].astype(F32) for dy in range(3))) for dx in range(3)]
        for a in range(2):
            for alpha in range(2):
                combined = split(*(by_column[dx][a, alpha] for dx in range(3)))
                for b in range(2):
                    for beta in range(2):
                        second_w[a, b, beta, at, alpha * 384 : (alpha + 1) * 384] = combined[b, beta].astype(BF16)
        return carry

    lax.fori_loop(0, 12, part, 0)
    for a in range(2):
        for b in range(2):
            for beta in range(2):
                second_w[a, b, beta, 192:256, :] = jnp.zeros((64, 768), BF16)


def convolve(c, me, latent, previous, first_w, conv_b, second_w, up_b, taps, wide, stage, ready):
    lane = lanes((64, 128))
    parity, frame, half_row = lax.rem(lane // 16, 2), lax.rem(lane // 8, 2), lax.rem(lane, 8)
    above = jnp.where(parity == 1, pltpu.roll(latent, 16, 1), jnp.where(half_row == 0, 0.0, pltpu.roll(latent, 113, 1)))
    below = jnp.where(parity == 0, pltpu.roll(latent, 112, 1), jnp.where(half_row == 7, 0.0, pltpu.roll(latent, 15, 1)))
    for r in range(2):
        at = slice(r * 16, r * 16 + 16)
        low = slice(32 + r * 16, 48 + r * 16)
        now = jnp.concatenate([above[low], latent[at], latent[low], below[at]], axis=0)
        before = previous[r]
        last = jnp.where(frame == 1, pltpu.roll(now, 8, 1), pltpu.roll(before, 120, 1))
        previous[r] = now
        one = jnp.transpose(jnp.concatenate([before, last], axis=0))
        two = jnp.transpose(jnp.concatenate([now, jnp.zeros((64, 128), F32)], axis=0))
        for place, w in enumerate((1, 2, 0, 3)):
            u = 2 * w + r
            part = slice(place * 32, place * 32 + 32)
            taps[u * 32 : u * 32 + 32, 0:128] = one[part].astype(BF16)
            taps[u * 32 : u * 32 + 32, 128:256] = two[part].astype(BF16)

    inner = rows((2, 8, 384))
    whole = conv_b
    for dx in range(3):
        whole = whole + jnp.dot(taps[dx * 32 : dx * 32 + 192, :], first_w[dx], preferred_element_type=F32)
    for m in range(6):
        hidden = whole[m * 32 : m * 32 + 32]
        if m == 0:
            hidden = jnp.where(me == 0, 0.0, hidden)
        if m == 5:
            hidden = jnp.where(me == GROUP - 1, 0.0, hidden)
        upper, lower = hidden[:, 0:384], hidden[:, 384:768]
        over = jnp.where(inner == 0, 0.0, pltpu.roll(lower[16:32].reshape(2, 8, 384), 1, 1)).reshape(16, 384)
        under = jnp.where(inner == 7, 0.0, pltpu.roll(upper[0:16].reshape(2, 8, 384), 7, 1)).reshape(16, 384)
        at = slice(m * 32, m * 32 + 32)
        over = jnp.concatenate([over, lower[0:16]], axis=0).astype(BF16)
        under = jnp.concatenate([upper[16:32], under], axis=0).astype(BF16)
        upper, lower = upper.astype(BF16), lower.astype(BF16)
        for q, parts in enumerate(((over, upper, lower), (upper, lower, under))):
            for i, value in enumerate(parts):
                wide[q, at, i * 384 : (i + 1) * 384] = value

    for a in range(2):
        for b in range(2):
            value = up_b
            for beta in range(2):
                left = wide[:, (b + beta) * 32 : (b + beta) * 32 + 128, a * 384 : a * 384 + 768].reshape(256, 768)
                value = value + lax.dot_general(left, second_w[a, b, beta], NT, preferred_element_type=F32)
            for q in range(2):
                for x in range(4):
                    at = (q * 4 + x) * 32
                    for half in range(2):
                        stage[half, pl.ds((q * 2 + a) * 256 + 2 * x + b, 32, stride=8), :] = value[
                            at : at + 32, half * 128 : (half + 1) * 128
                        ]
    for p in range(4):
        for parity in range(2):
            for f in range(2):
                at = pl.ds(p * 256 + parity * 128 + f * 64, 64)
                ready[c, f, :, parity, p, :, 0:128] = stage[0, at, :].reshape(8, 8, 128).astype(BF16)
                ready[c, f, :, parity, p, :, 128:192] = stage[1, at, :].reshape(8, 8, 128)[:, :, 0:64].astype(BF16)


def kernel(
    x_hbm, shift_ref, scale_ref, head_w_ref, head_b_ref, lat_mean_ref, lat_std_ref,
    conv_w_ref, conv_b_ref, up_w_ref, up_b_ref,
    out_hbm,
    x_buf, partial, sums, turned, own_stat, peer_stat, rest, give, got, parcel, arrived, stat_out, stat_in,
    sent, beside, conv_w, up_w, first_w, second_w, previous, taps, wide, stage, ready,
    x_sem, w_sem, stat_sem, core_send, core_recv, send_sem, recv_sem, ssend_sem, srecv_sem, hsend_sem, hrecv_sem,
    out_sem,
):
    me = lax.axis_index("sp")
    req = lax.axis_index("req")
    core = lax.rem(me, 2)
    chip = me // 2
    y, z = chip // 8, lax.rem(chip, 8)
    chips = [lax.rem(y + dy, 2) * 8 + lax.rem(z + dz, 8) for dy, dz in OFFSETS]
    partner = (req, chip * 2 + (1 - core))
    left, right = lax.rem(me + GROUP - 1, GROUP), lax.rem(me + 1, GROUP)
    other = jnp.where(core == 0, left, right)

    def remote(src, dst, send, recv, to):
        return pltpu.make_async_remote_copy(
            src_ref=src, dst_ref=dst, send_sem=send, recv_sem=recv, device_id=to, device_id_type=MESH
        )

    x_copies = []
    for c in range(CHUNKS):
        copy = pltpu.make_async_copy(x_hbm.at[:, pl.ds(c * 2048, 2048)], x_buf.at[c], x_sem.at[c])
        copy.start()
        x_copies.append(copy)
    conv_copy = pltpu.make_async_copy(conv_w_ref, conv_w, w_sem.at[0])
    up_copy = pltpu.make_async_copy(up_w_ref, up_w, w_sem.at[1])
    conv_copy.start()
    up_copy.start()

    barrier = pltpu.get_barrier_semaphore()
    for to in chips[:-1]:
        pl.semaphore_signal(barrier, inc=1, device_id=(req, to * 2 + core), device_id_type=MESH)
    pl.semaphore_signal(barrier, inc=1, device_id=partner, device_id_type=MESH)
    pl.semaphore_signal(barrier, inc=1, device_id=(req, other), device_id_type=MESH)

    head = head_w_ref[...].astype(F32)
    folded = (1.0 + scale_ref[...].reshape(1, LOCAL)) * head
    weight_sum = jnp.sum(folded, axis=1, keepdims=True)
    shifted = jnp.sum(shift_ref[...].reshape(1, LOCAL) * head, axis=1, keepdims=True)
    centred = folded - weight_sum * (1.0 / LOCAL)
    high = centred.astype(BF16)
    low = (centred - high.astype(F32)).astype(BF16)
    weights = jnp.concatenate([high, low, jnp.ones((16, LOCAL), BF16)], axis=0)

    def core_copy(c):
        return remote(give.at[c], got.at[c], core_send.at[c], core_recv.at[c], partner)

    def gathered(c, to, core_to):
        at = (to * 2 + core_to) * 2
        return jnp.concatenate(
            [
                partial[c, pl.ds(parity * 64 + at + column, 8, stride=128), :]
                for column in range(2)
                for parity in range(2)
            ],
            axis=0,
        )

    def parcel_copy(c, k):
        return remote(
            parcel.at[c, k], arrived.at[c, k], send_sem.at[c, k], recv_sem.at[c, k], (req, chips[k] * 2 + core)
        )

    def dispatch(c):
        core_copy(c).wait_recv()
        for k in range(CHIPS):
            merged = gathered(c, chips[k], core) + got[c, k].astype(F32)
            if k == CHIPS - 1:
                rest[c] = merged
            else:
                parcel[c, k] = merged.astype(BF16)
                parcel_copy(c, k).start()

    for c in range(CHUNKS):
        x_copies[c].wait()

        def block(i, carry):
            products = []
            for f in range(2):
                x = x_buf[c, :, pl.ds(pl.multiple_of(f * 1024 + i * 256, 256), 256)]
                product = jnp.dot(weights, x, preferred_element_type=F32)
                products.append(product[0:64] + product[64:128])
                wide_x = x.astype(F32)
                power = jnp.sum(wide_x * wide_x, axis=0, keepdims=True)
                for half in range(2):
                    at = (c * 2 + f) * 8 + i * 2 + half
                    cut = slice(half * 128, half * 128 + 128)
                    sums[pl.ds(at, 1), :] = product[128:129, cut]
                    sums[pl.ds(64 + at, 1), :] = power[:, cut]
            for half in range(2):
                cut = slice(half * 128, half * 128 + 128)
                pair = jnp.concatenate([products[0][:, cut], products[1][:, cut]], axis=0)
                partial[c, pl.ds(pl.multiple_of((i * 2 + half) * 128, 128), 128), :] = jnp.transpose(pair)
            return carry

        lax.fori_loop(0, 4, block, 0, unroll=True)
        if c == 0:
            pl.semaphore_wait(barrier, 17)
        for k in range(CHIPS):
            give[c, k] = gathered(c, chips[k], 1 - core).astype(BF16)
        core_copy(c).start()

    turned[0:128, :] = jnp.transpose(sums[...])
    group = lax.rem(lanes((32, 128)) // 16, 4)
    quarters = [turned[pl.ds(parity * 64 + column, 32, stride=2), :] for column in range(2) for parity in range(2)]
    for c in range(CHUNKS):
        placed = [quarters[g] if g == c else pltpu.roll(quarters[g], (16 * (g - c)) % 128, 1) for g in range(4)]
        own_stat[c] = jnp.where(
            group == 0, placed[0], jnp.where(group == 1, placed[1], jnp.where(group == 2, placed[2], placed[3]))
        )
    own_row = jnp.concatenate([to_row(weight_sum), to_row(shifted)], axis=1)
    own_stat[4] = jnp.broadcast_to(own_row, (32, 128))
    stat_copy = remote(own_stat, peer_stat, stat_sem.at[0], stat_sem.at[1], partner)
    stat_copy.start()
    dispatch(0)
    stat_copy.wait()

    low_half = lanes((32, 128)) < 64
    own = [own_stat[c] for c in range(5)]
    peer = [peer_stat[c] for c in range(5)]
    both = [own[c] + peer[c] for c in range(5)]
    turned_both = [pltpu.roll(both[c], 64, 1) for c in range(5)]
    lines = [jnp.where(low_half, own[c], pltpu.roll(peer[c], 64, 1)) for c in range(5)]
    lines = lines[0:4] + [
        jnp.where(low_half, turned_both[0], both[1]), jnp.where(low_half, turned_both[2], both[3]),
        lines[4], turned_both[4],
    ]
    for line in range(8):
        turned[pl.ds(line, 32, stride=8), :] = lines[line]

    def stat_remote(k):
        return remote(
            stat_out.at[k], stat_in.at[pl.ds(k * 8, 8)], ssend_sem.at[k], srecv_sem.at[k], (req, chips[k] * 2 + core)
        )

    for k in range(CHIPS):
        value = turned[pl.ds(pl.multiple_of((chips[k] * 2 + core) * 8, 8), 8), :]
        if k == CHIPS - 1:
            stat_in[k * 8 : k * 8 + 8, :] = value
        else:
            stat_out[k] = value
            stat_remote(k).start()

    dispatch(1)
    conv_copy.wait()
    prepare_first(conv_w, first_w)
    up_copy.wait()
    prepare_second(up_w, second_w)
    previous[...] = jnp.zeros((2, 64, 128), F32)

    for k in range(CHIPS - 1):
        stat_remote(k).wait_recv()
    total = jnp.sum(stat_in[...].reshape(CHIPS, 8, 128), axis=0)
    sums_of = [stat_in[pl.ds(c, CHIPS, stride=8), :] for c in range(4)]
    heads = stat_in[pl.ds(6, CHIPS, stride=8), :]
    heads = jnp.concatenate([heads, pltpu.roll(heads, 64, 1), jnp.zeros((96, 128), F32)], axis=0)
    heads = jnp.transpose(heads)[0:64, :]
    both_sums = total + pltpu.roll(total, 64, 1)
    means = both_sums[0:4] * (1.0 / FEATS)
    swapped = pltpu.roll(total, 64, 1)
    bias = to_column(total[7:8, 0:64] + head_b_ref[...].reshape(1, 64))
    std = to_column(tile16(lat_std_ref[...].reshape(1, 16)))
    shift = to_column(tile16(lat_mean_ref[...].reshape(1, 16)))
    centres, scales = [], []
    for c in range(CHUNKS):
        mean = means[c : c + 1]
        off = sums_of[c] * (1.0 / LOCAL) - mean
        off = jnp.concatenate([off, pltpu.roll(off, 64, 1), jnp.zeros((96, 128), F32)], axis=0)
        centres.append(jnp.dot(heads, off, precision=lax.Precision.HIGHEST, preferred_element_type=F32))
        power = (total if c % 2 == 0 else swapped)[4 + c // 2 : 5 + c // 2]
        scales.append(lax.rsqrt(power * (1.0 / FEATS) - mean * mean + 1e-06))

    lane = lanes((64, 128))
    conv_b = conv_b_ref[...].reshape(1, 384)
    conv_b = jnp.concatenate([conv_b, conv_b], axis=1)
    up_b = jnp.concatenate([up_b_ref[...].reshape(1, 192), jnp.zeros((1, 64), F32)], axis=1)

    def halo_copies(c):
        return [
            remote(sent.at[c], beside.at[c, side], hsend_sem.at[c, side], hrecv_sem.at[c, side], (req, to))
            for side, to in ((1, left), (0, right))
        ]

    def finish(c):
        for k in range(CHIPS - 1):
            parcel_copy(c, k).wait_recv()
        value = rest[c]
        for k in range(CHIPS - 1):
            value = value + arrived[c, k].astype(F32)
        none = jnp.zeros((8, 128), F32)
        spread = []
        for g in range(4):
            spread += [value[g * 8 : g * 8 + 8], none]
        value = jnp.transpose(jnp.concatenate(spread + [jnp.zeros((64, 128), F32)], axis=0))
        value = jnp.where(lax.rem(lane // 8, 2) == 0, value[0:64], pltpu.roll(value[64:128], 8, 1))
        patches = (value + centres[c]) * scales[c] + bias
        sent[c] = (patches * std + shift).astype(BF16)
        for copy in halo_copies(c):
            copy.start()

    def decode(c):
        for copy in halo_copies(c):
            copy.wait_recv()
        own = sent[c].astype(F32)
        before = jnp.where(me == 0, 0.0, pltpu.roll(beside[c, 0].astype(F32), 32, 1))
        after = jnp.where(me == GROUP - 1, 0.0, pltpu.roll(beside[c, 1].astype(F32), 96, 1))
        latent = jnp.where(lane < 64, own, jnp.where(lane < 96, before, after))
        convolve(c, me, latent, previous, first_w, conv_b, second_w, up_b, taps, wide, stage, ready)
        pltpu.make_async_copy(ready.at[c], out_hbm.at[pl.ds(2 * c, 2)], out_sem.at[c]).start()

    finish(0)
    dispatch(2)
    finish(1)
    dispatch(3)
    decode(0)
    finish(2)
    decode(1)
    finish(3)
    decode(2)
    decode(3)

    for c in range(CHUNKS):
        pltpu.make_async_copy(ready.at[c], out_hbm.at[pl.ds(2 * c, 2)], out_sem.at[c]).wait()
        core_copy(c).wait_send()
        for k in range(CHIPS - 1):
            parcel_copy(c, k).wait_send()
        for copy in halo_copies(c):
            copy.wait_send()
    for k in range(CHIPS - 1):
        stat_remote(k).wait_send()


def shards(
    hidden_feats, mod_shift, mod_scale, head_w, head_b, latent_mean, latent_std, conv_in_w, conv_in_b, up_w, up_b
):
    vmem = pl.BlockSpec(memory_space=pltpu.VMEM)
    hbm = pl.BlockSpec(memory_space=pltpu.HBM)
    dma = pltpu.SemaphoreType.DMA
    decoded = pl.pallas_call(
        kernel,
        out_shape=jax.ShapeDtypeStruct((8, 8, 2, 4, 8, 192), BF16),
        in_specs=[hbm] + [vmem] * 6 + [hbm, vmem, hbm, vmem],
        out_specs=hbm,
        scratch_shapes=[
            pltpu.VMEM((CHUNKS, LOCAL, 2048), BF16),
            pltpu.VMEM((CHUNKS, 1024, 128), F32),
            pltpu.VMEM((128, 128), F32),
            pltpu.VMEM((256, 128), F32),
            pltpu.VMEM((5, 32, 128), F32),
            pltpu.VMEM((5, 32, 128), F32),
            pltpu.VMEM((CHUNKS, 32, 128), F32),
            pltpu.VMEM((CHUNKS, CHIPS, 32, 128), BF16),
            pltpu.VMEM((CHUNKS, CHIPS, 32, 128), BF16),
            pltpu.VMEM((CHUNKS, CHIPS, 32, 128), BF16),
            pltpu.VMEM((CHUNKS, CHIPS, 32, 128), BF16),
            pltpu.VMEM((CHIPS, 8, 128), F32),
            pltpu.VMEM((CHIPS * 8, 128), F32),
            pltpu.VMEM((CHUNKS, 64, 128), BF16),
            pltpu.VMEM((CHUNKS, 2, 64, 128), BF16),
            pltpu.VMEM((3, 3, 3, 16, 384), BF16),
            pltpu.VMEM((3, 3, 192, 384), BF16),
            pltpu.VMEM((3, 256, 768), BF16),
            pltpu.VMEM((2, 2, 2, 256, 768), BF16),
            pltpu.VMEM((2, 64, 128), F32),
            pltpu.VMEM((256, 256), BF16),
            pltpu.VMEM((2, 192, 1152), BF16),
            pltpu.VMEM((2, 1024, 128), F32),
            pltpu.VMEM((CHUNKS, 2, 8, 2, 4, 8, 192), BF16),
            dma((CHUNKS,)),
            dma((2,)),
            dma((2,)),
            dma((CHUNKS,)),
            dma((CHUNKS,)),
            dma((CHUNKS, CHIPS)),
            dma((CHUNKS, CHIPS)),
            dma((CHIPS,)),
            dma((CHIPS,)),
            dma((CHUNKS, 2)),
            dma((CHUNKS, 2)),
            dma((CHUNKS,)),
        ],
        compiler_params=pltpu.CompilerParams(
            collective_id=0, has_side_effects=True, vmem_limit_bytes=62 * 1024 * 1024
        ),
        name="decode",
    )(
        hidden_feats.T, mod_shift, mod_scale, head_w.T, head_b, latent_mean, latent_std,
        conv_in_w, conv_in_b, jnp.swapaxes(up_w, 2, 3), up_b,
    )
    return decoded.reshape(8, 64, 8, 192)


def solution(mesh):
    placed = (
        P("req", "sp"),
        P(("req", "sp")),
        P(("req", "sp")),
        P("sp", None),
        P(),
        P(),
        P(),
        P(),
        P(),
        P(),
        P(),
    )
    return jax.shard_map(
        shards, mesh=mesh, in_specs=placed, out_specs=P("req", None, "sp", None), check_vma=False
    )
```

time: 431 us -> 42.4 us (0.10)
  waiting for transfers between devices: 357 us -> 0 us
  Pallas kernels: 0 us -> 39.2 us
  blocking collectives: 20.8 us -> 0 us
  matrix products: 16.4 us -> 0 us
  between operations: 13.7 us -> 0.01 us
  starting transfers between devices: 9.54 us -> 0 us
  other arithmetic: 5.7 us -> 0 us
    psum x1 -> x0, waiting for transfers between devices: 236 us -> none  [shards(): lax.psum((jnp.sum(feats, axis=1), jnp.sum(feats * feats, axis=1)), 'sp')]
    reduce_scatter x1 -> x0, waiting for transfers between devices: 111 us -> none  [shards(): lax.psum_scatter(jnp.dot(normed, head_w, preferred_element_type=jnp.float...]
    pallas_call x0 -> x1, Pallas kernels: none -> 39.2 us  [shards(): pl.pallas_call(kernel, out_shape=jax.ShapeDtypeStruct((8, 8, 2, 4, 8, 192...]
    all_to_all x1 -> x0, blocking collectives: 20.8 us -> none  [shards(): lax.all_to_all(pieces, 'sp', split_axis=1, concat_axis=0, tiled=True)]
    conv_general_dilated x2 -> x0, matrix products: 12 us -> none  [the longest x1 8.11 us: second_conv(): lax.conv_general_dilated(padded, up_w, (1, 1), 'VALID', dimension_numbers...]
    ppermute x4 -> x0, waiting for transfers between devices: 10.1 us -> none  [the longest x2 8.04 us: padded_2(): lax.ppermute(lax.slice_in_dim(block, 0, width, axis=dim), axis, backward)]
    ppermute x4 -> x0, starting transfers between devices: 9.47 us -> none  [the longest x2 4.94 us: padded_2(): lax.ppermute(lax.slice_in_dim(block, block.shape[dim] - width, None, axis...]
    dot_general x1 -> x0, matrix products: 4.34 us -> none  [shards(): jnp.dot(normed, head_w, preferred_element_type=jnp.float32)]
  transfers between devices with their start and end apart: 6 -> 0, of which waited for: 5 -> 0; matrix products, arithmetic and copies ran while one was open for 0% -> 0% of each run, Pallas kernels for 0% -> 0%
where the time goes in v2:
time: 42.4 us; the launch traced here: 42.2 us
  Pallas kernels  39.2 us (92%)
  local copies, waits for them, and re-layouts  3.05 us (7%)
    pallas_call x1, Pallas kernels, shards(): pl.pallas_call(kernel, out_shape=jax.ShapeDtypeStruct((8, 8, 2, 4, 8, 192...  39.2 us
    unnamed x1, local copies, waits for them, and re-layouts  3.05 us

profile of v2, /device:TPU:1, one launch (start us, length us, event | category | flops | bytes accessed | tf_op | source)
XLA Modules:
  0.0 42.2 jit_solution(11270339396446298470)
XLA Ops:
  0.0 39.2 %decode.1 = bf16[8,8,2,4,8,192]{5,4,3,2,1,0:T(8,128)(2,1)} custom-call(bf16[160,8192]{1,0:T(8,128)(2,1)} %bitcast.5, f32[160]{0:T(256)} %shift_ref.1, f32[160]{0:T(256)} %scale_ref.1, bf16[64,160]{1,0:T(8,128)(2,1)} %bitcast.7, f32[64]{0:T(128)} %head_b_ref.1, f32[16]{0:T(128)} %lat_mean_ref.1, f32[16]{0:T(128)} %lat_std_ref.1, ...), custom_call_target="tpu_custom_call" | custom-call | tf_op jit(solution)/shard_map/decode/pallas_call | solution.py:387
  39.2 3.0 %copy.13 = bf16[8,64,8,192]{3,2,1,0:T(8,128)(2,1)} copy(bf16[8,64,8,192]{3,2,1,0:T(8,128)(2,1)} %bitcast.4) | data formatting | bytes 3145728

commit v3 on v2

--- a/solution.py
+++ b/solution.py
@@ -79,7 +79,7 @@
                 second_w[a, b, beta, 192:256, :] = jnp.zeros((64, 768), BF16)
 
 
-def convolve(c, me, latent, previous, first_w, conv_b, second_w, up_b, taps, wide, stage, ready):
+def first_convolution(me, latent, previous, first_w, conv_b, taps, wide):
     lane = lanes((64, 128))
     parity, frame, half_row = lax.rem(lane // 16, 2), lax.rem(lane // 8, 2), lax.rem(lane, 8)
     above = jnp.where(parity == 1, pltpu.roll(latent, 16, 1), jnp.where(half_row == 0, 0.0, pltpu.roll(latent, 113, 1)))
@@ -120,7 +120,11 @@
             for i, value in enumerate(parts):
                 wide[q, at, i * 384 : (i + 1) * 384] = value
 
+
+def second_convolution(second_w, up_b, wide, stage, ready, between=None):
     for a in range(2):
+        if a == 1 and between is not None:
+            between()
         for b in range(2):
             value = up_b
             for beta in range(2):
@@ -137,18 +141,19 @@
         for parity in range(2):
             for f in range(2):
                 at = pl.ds(p * 256 + parity * 128 + f * 64, 64)
-                ready[c, f, :, parity, p, :, 0:128] = stage[0, at, :].reshape(8, 8, 128).astype(BF16)
-                ready[c, f, :, parity, p, :, 128:192] = stage[1, at, :].reshape(8, 8, 128)[:, :, 0:64].astype(BF16)
-
-
-def kernel(
-    x_hbm, shift_ref, scale_ref, head_w_ref, head_b_ref, lat_mean_ref, lat_std_ref,
-    conv_w_ref, conv_b_ref, up_w_ref, up_b_ref,
-    out_hbm,
+                ready[f, :, parity, p, :, 0:128] = stage[0, at, :].reshape(8, 8, 128).astype(BF16)
+                ready[f, :, parity, p, :, 128:192] = stage[1, at, :].reshape(8, 8, 128)[:, :, 0:64].astype(BF16)
+
+
+def reduce_kernel(
+    x_hbm, shift_hbm, scale_hbm, head_w_hbm, head_b_hbm, lat_mean_hbm, lat_std_hbm,
+    conv_w_hbm, conv_b_hbm, up_w_hbm, up_b_hbm,
+    out_hbm, state_hbm, first_hbm, second_hbm,
     x_buf, partial, sums, turned, own_stat, peer_stat, rest, give, got, parcel, arrived, stat_out, stat_in,
-    sent, beside, conv_w, up_w, first_w, second_w, previous, taps, wide, stage, ready,
+    sent, beside, conv_w, up_w, first_w, second_w, previous, taps, wide, stage, ready, state,
+    shift_ref, scale_ref, head_w_ref, head_b_ref, lat_mean_ref, lat_std_ref, conv_b_ref, up_b_ref,
     x_sem, w_sem, stat_sem, core_send, core_recv, send_sem, recv_sem, ssend_sem, srecv_sem, hsend_sem, hrecv_sem,
-    out_sem,
+    out_sem, keep_sem, small_sem,
 ):
     me = lax.axis_index("sp")
     req = lax.axis_index("req")
@@ -165,15 +170,18 @@
             src_ref=src, dst_ref=dst, send_sem=send, recv_sem=recv, device_id=to, device_id_type=MESH
         )
 
+    pairs = (
+        (shift_hbm, shift_ref), (scale_hbm, scale_ref), (head_w_hbm, head_w_ref), (head_b_hbm, head_b_ref),
+        (lat_mean_hbm, lat_mean_ref), (lat_std_hbm, lat_std_ref), (conv_b_hbm, conv_b_ref), (up_b_hbm, up_b_ref),
+    )
+    small = [pltpu.make_async_copy(src, dst, small_sem.at[i]) for i, (src, dst) in enumerate(pairs)]
+    for copy in small:
+        copy.start()
     x_copies = []
     for c in range(CHUNKS):
         copy = pltpu.make_async_copy(x_hbm.at[:, pl.ds(c * 2048, 2048)], x_buf.at[c], x_sem.at[c])
         copy.start()
         x_copies.append(copy)
-    conv_copy = pltpu.make_async_copy(conv_w_ref, conv_w, w_sem.at[0])
-    up_copy = pltpu.make_async_copy(up_w_ref, up_w, w_sem.at[1])
-    conv_copy.start()
-    up_copy.start()
 
     barrier = pltpu.get_barrier_semaphore()
     for to in chips[:-1]:
@@ -181,6 +189,13 @@
     pl.semaphore_signal(barrier, inc=1, device_id=partner, device_id_type=MESH)
     pl.semaphore_signal(barrier, inc=1, device_id=(req, other), device_id_type=MESH)
 
+    conv_copy = pltpu.make_async_copy(conv_w_hbm, conv_w, w_sem.at[0])
+    up_copy = pltpu.make_async_copy(up_w_hbm, up_w, w_sem.at[1])
+    conv_copy.start()
+    up_copy.start()
+
+    for copy in small:
+        copy.wait()
     head = head_w_ref[...].astype(F32)
     folded = (1.0 + scale_ref[...].reshape(1, LOCAL)) * head
     weight_sum = jnp.sum(folded, axis=1, keepdims=True)
@@ -242,8 +257,8 @@
             return carry
 
         lax.fori_loop(0, 4, block, 0, unroll=True)
-        if c == 0:
-            pl.semaphore_wait(barrier, 17)
+    pl.semaphore_wait(barrier, 17)
+    for c in range(CHUNKS):
         for k in range(CHIPS):
             give[c, k] = gathered(c, chips[k], 1 - core).astype(BF16)
         core_copy(c).start()
@@ -290,11 +305,18 @@
             stat_remote(k).start()
 
     dispatch(1)
+    dispatch(2)
     conv_copy.wait()
     prepare_first(conv_w, first_w)
     up_copy.wait()
     prepare_second(up_w, second_w)
     previous[...] = jnp.zeros((2, 64, 128), F32)
+    keeps = [
+        pltpu.make_async_copy(first_w, first_hbm, keep_sem.at[0]),
+        pltpu.make_async_copy(second_w, second_hbm, keep_sem.at[1]),
+    ]
+    for copy in keeps:
+        copy.start()
 
     for k in range(CHIPS - 1):
         stat_remote(k).wait_recv()
@@ -329,6 +351,11 @@
             for side, to in ((1, left), (0, right))
         ]
 
+    def ends(c, action):
+        to_left, to_right = halo_copies(c)
+        pl.when(me > 0)(getattr(to_left, action))
+        pl.when(me < GROUP - 1)(getattr(to_right, action))
+
     def finish(c):
         for k in range(CHIPS - 1):
             parcel_copy(c, k).wait_recv()
@@ -343,52 +370,110 @@
         value = jnp.where(lax.rem(lane // 8, 2) == 0, value[0:64], pltpu.roll(value[64:128], 8, 1))
         patches = (value + centres[c]) * scales[c] + bias
         sent[c] = (patches * std + shift).astype(BF16)
-        for copy in halo_copies(c):
-            copy.start()
-
-    def decode(c):
-        for copy in halo_copies(c):
-            copy.wait_recv()
+        ends(c, "start")
+
+    def assembled(c):
+        pl.when(me > 0)(halo_copies(c)[1].wait_recv)
+        pl.when(me < GROUP - 1)(halo_copies(c)[0].wait_recv)
         own = sent[c].astype(F32)
         before = jnp.where(me == 0, 0.0, pltpu.roll(beside[c, 0].astype(F32), 32, 1))
         after = jnp.where(me == GROUP - 1, 0.0, pltpu.roll(beside[c, 1].astype(F32), 96, 1))
-        latent = jnp.where(lane < 64, own, jnp.where(lane < 96, before, after))
-        convolve(c, me, latent, previous, first_w, conv_b, second_w, up_b, taps, wide, stage, ready)
-        pltpu.make_async_copy(ready.at[c], out_hbm.at[pl.ds(2 * c, 2)], out_sem.at[c]).start()
+        return jnp.where(lane < 64, own, jnp.where(lane < 96, before, after))
+
+    def out_copy(c):
+        return pltpu.make_async_copy(ready.at[c], out_hbm.at[pl.ds(2 * c, 2)], out_sem.at[c])
+
+    def decode(c):
+        latent = assembled(c)
+        first_convolution(me, latent, previous, first_w, conv_b, taps, wide)
+        second_convolution(second_w, up_b, wide, stage, ready.at[c])
+        out_copy(c).start()
 
     finish(0)
-    dispatch(2)
+    dispatch(3)
     finish(1)
-    dispatch(3)
     decode(0)
     finish(2)
     decode(1)
     finish(3)
     decode(2)
-    decode(3)
-
+
+    state[2] = assembled(CHUNKS - 1)
+    state[0:2] = previous[...]
+    for i in range(6):
+        state[3, i : i + 1, :] = conv_b[:, i * 128 : (i + 1) * 128]
+    for i in range(2):
+        state[3, 8 + i : 9 + i, :] = up_b[:, i * 128 : (i + 1) * 128]
+    keeps.append(pltpu.make_async_copy(state, state_hbm, keep_sem.at[2]))
+    keeps[2].start()
     for c in range(CHUNKS):
-        pltpu.make_async_copy(ready.at[c], out_hbm.at[pl.ds(2 * c, 2)], out_sem.at[c]).wait()
+        if c < CHUNKS - 1:
+            out_copy(c).wait()
         core_copy(c).wait_send()
         for k in range(CHIPS - 1):
             parcel_copy(c, k).wait_send()
-        for copy in halo_copies(c):
-            copy.wait_send()
+        ends(c, "wait_send")
     for k in range(CHIPS - 1):
         stat_remote(k).wait_send()
+    for copy in keeps:
+        copy.wait()
+
+
+def last_kernel(
+    done_hbm, state_hbm, first_hbm, second_hbm,
+    out_hbm,
+    done, state, first_w, second_w, previous, taps, wide, stage, ready, sem,
+):
+    me = lax.axis_index("sp")
+    frames = 2 * (CHUNKS - 1)
+    load_state = pltpu.make_async_copy(state_hbm, state, sem.at[0])
+    load_first = pltpu.make_async_copy(first_hbm, first_w, sem.at[1])
+    load_second = pltpu.make_async_copy(second_hbm, second_w, sem.at[2])
+    load_done = pltpu.make_async_copy(done_hbm, done, sem.at[3])
+    for copy in (load_state, load_first, load_second, load_done):
+        copy.start()
+    load_state.wait()
+    previous[...] = state[0:2]
+    conv_b = jnp.concatenate([state[3, i : i + 1, :] for i in range(6)], axis=1)
+    up_b = jnp.concatenate([state[3, i : i + 1, :] for i in (8, 9)], axis=1)
+    load_first.wait()
+    first_convolution(me, state[2], previous, first_w, conv_b, taps, wide)
+    load_second.wait()
+    store_done = pltpu.make_async_copy(done, out_hbm.at[pl.ds(0, frames)], sem.at[4])
+
+    def between():
+        load_done.wait()
+        store_done.start()
+
+    second_convolution(second_w, up_b, wide, stage, ready, between)
+    store = pltpu.make_async_copy(ready, out_hbm.at[pl.ds(frames, 2)], sem.at[5])
+    store.start()
+    store_done.wait()
+    store.wait()
 
 
 def shards(
     hidden_feats, mod_shift, mod_scale, head_w, head_b, latent_mean, latent_std, conv_in_w, conv_in_b, up_w, up_b
 ):
-    vmem = pl.BlockSpec(memory_space=pltpu.VMEM)
     hbm = pl.BlockSpec(memory_space=pltpu.HBM)
     dma = pltpu.SemaphoreType.DMA
-    decoded = pl.pallas_call(
-        kernel,
-        out_shape=jax.ShapeDtypeStruct((8, 8, 2, 4, 8, 192), BF16),
-        in_specs=[hbm] + [vmem] * 6 + [hbm, vmem, hbm, vmem],
-        out_specs=hbm,
+    pieces = jax.ShapeDtypeStruct((8, 8, 2, 4, 8, 192), BF16)
+    work = [
+        pltpu.VMEM((2, 64, 128), F32),
+        pltpu.VMEM((256, 256), BF16),
+        pltpu.VMEM((2, 192, 1152), BF16),
+        pltpu.VMEM((2, 1024, 128), F32),
+    ]
+    held = [
+        jax.ShapeDtypeStruct((4, 64, 128), F32),
+        jax.ShapeDtypeStruct((3, 256, 768), BF16),
+        jax.ShapeDtypeStruct((2, 2, 2, 256, 768), BF16),
+    ]
+    done, state, first_w, second_w = pl.pallas_call(
+        reduce_kernel,
+        out_shape=[jax.ShapeDtypeStruct((6, 8, 2, 4, 8, 192), BF16)] + held,
+        in_specs=[hbm] * 11,
+        out_specs=[hbm] * 4,
         scratch_shapes=[
             pltpu.VMEM((CHUNKS, LOCAL, 2048), BF16),
             pltpu.VMEM((CHUNKS, 1024, 128), F32),
@@ -409,11 +494,17 @@
             pltpu.VMEM((3, 3, 192, 384), BF16),
             pltpu.VMEM((3, 256, 768), BF16),
             pltpu.VMEM((2, 2, 2, 256, 768), BF16),
-            pltpu.VMEM((2, 64, 128), F32),
-            pltpu.VMEM((256, 256), BF16),
-            pltpu.VMEM((2, 192, 1152), BF16),
-            pltpu.VMEM((2, 1024, 128), F32),
-            pltpu.VMEM((CHUNKS, 2, 8, 2, 4, 8, 192), BF16),
+            *work,
+            pltpu.VMEM((CHUNKS - 1, 2, 8, 2, 4, 8, 192), BF16),
+            pltpu.VMEM((4, 64, 128), F32),
+            pltpu.VMEM((LOCAL,), F32),
+            pltpu.VMEM((LOCAL,), F32),
+            pltpu.VMEM((64, LOCAL), BF16),
+            pltpu.VMEM((64,), F32),
+            pltpu.VMEM((16,), F32),
+            pltpu.VMEM((16,), F32),
+            pltpu.VMEM((384,), F32),
+            pltpu.VMEM((192,), F32),
             dma((CHUNKS,)),
             dma((2,)),
             dma((2,)),
@@ -426,15 +517,34 @@
             dma((CHUNKS, 2)),
             dma((CHUNKS, 2)),
             dma((CHUNKS,)),
+            dma((3,)),
+            dma((8,)),
         ],
         compiler_params=pltpu.CompilerParams(
             collective_id=0, has_side_effects=True, vmem_limit_bytes=62 * 1024 * 1024
         ),
-        name="decode",
+        name="reduce",
     )(
         hidden_feats.T, mod_shift, mod_scale, head_w.T, head_b, latent_mean, latent_std,
         conv_in_w, conv_in_b, jnp.swapaxes(up_w, 2, 3), up_b,
     )
+    decoded = pl.pallas_call(
+        last_kernel,
+        out_shape=pieces,
+        in_specs=[hbm] * 4,
+        out_specs=hbm,
+        scratch_shapes=[
+            pltpu.VMEM((6, 8, 2, 4, 8, 192), BF16),
+            pltpu.VMEM((4, 64, 128), F32),
+            pltpu.VMEM((3, 256, 768), BF16),
+            pltpu.VMEM((2, 2, 2, 256, 768), BF16),
+            *work,
+            pltpu.VMEM((2, 8, 2, 4, 8, 192), BF16),
+            dma((6,)),
+        ],
+        compiler_params=pltpu.CompilerParams(vmem_limit_bytes=62 * 1024 * 1024),
+        name="last",
+    )(done, state, first_w, second_w)
     return decoded.reshape(8, 64, 8, 192)
 
 

time: 42.4 us -> 39.2 us (0.925)
  local copies, waits for them, and re-layouts: 3.05 us -> 0 us
    unnamed x1 -> x0, local copies, waits for them, and re-layouts: 3.05 us -> none
    pallas_call x1 -> x2, Pallas kernels: 39.2 us -> 39.1 us  [the longest x1 34.5 us: shards(): pl.pallas_call(reduce_kernel, out_shape=[jax.ShapeDtypeStruct((6, 8, 2, 4...]
where the time goes in v3:
time: 39.2 us; the launch traced here: 39.1 us
  Pallas kernels  39.1 us (100%)
    pallas_call x1, Pallas kernels, shards(): pl.pallas_call(reduce_kernel, out_shape=[jax.ShapeDtypeStruct((6, 8, 2, 4...  34.5 us
    pallas_call x1, Pallas kernels, shards(): pl.pallas_call(last_kernel, out_shape=pieces, in_specs=[hbm] * 4, out_spe...  4.59 us

profile of v3, /device:TPU:1, one launch (start us, length us, event | category | flops | bytes accessed | tf_op | source)
XLA Modules:
  0.0 39.1 jit_solution(8427735278229218802)
XLA Ops:
  0.0 34.5 %reduce.1 = (bf16[6,8,2,4,8,192]{5,4,3,2,1,0:T(8,128)(2,1)}, f32[4,64,128]{2,1,0:T(8,128)}, bf16[3,256,768]{2,1,0:T(8,128)(2,1)}, bf16[2,2,2,256,768]{4,3,2,1,0:T(8,128)(2,1)}) custom-call(bf16[160,8192]{1,0:T(8,128)(2,1)} %bitcast.4, f32[160]{0:T(256)} %shift_hbm.1, f32[160]{0:T(256)} %scale_hbm.1, bf16[64,160]{1,0:T(8,128)(2,1)} %bitcast.6, f32[64]{0:T(128)} %head_b_hbm.1, ...), custom_call_target="tpu_custom_call" | custom-call | tf_op jit(solution)/shard_map/reduce/pallas_call | solution.py:472
  34.5 4.6 %last.1 = bf16[8,8,2,4,8,192]{5,4,3,2,1,0:T(8,128)(2,1)} custom-call(bf16[6,8,2,4,8,192]{5,4,3,2,1,0:T(8,128)(2,1)} %get-tuple-element.9.done_hbm, f32[4,64,128]{2,1,0:T(8,128)} %get-tuple-element.10.state_hbm, bf16[3,256,768]{2,1,0:T(8,128)(2,1)} %get-tuple-element.11.first_hbm, bf16[2,2,2,256,768]{4,3,2,1,0:T(8,128)(2,1)} %get-tuple-element.12.second_hbm), custom_call_target="tpu_custom_call" | custom-call | tf_op jit(solution)/shard_map/last/pallas_call | solution.py:531

commit v4 on v3

--- a/solution.py
+++ b/solution.py
@@ -14,7 +14,9 @@
 CHUNKS = 4
 CHIPS = 16
 GROUP = 32
+FAR = 6
 OFFSETS = [(dy, dz) for dz in (4, 3, 5, 2, 6, 1, 7) for dy in (1, 0)] + [(1, 0), (0, 0)]
+SLOTS = (*range(1, FAR, 2), *range(FAR, CHIPS - 1))
 NT = (((1,), (1,)), ((), ()))
 
 
@@ -149,11 +151,11 @@
     x_hbm, shift_hbm, scale_hbm, head_w_hbm, head_b_hbm, lat_mean_hbm, lat_std_hbm,
     conv_w_hbm, conv_b_hbm, up_w_hbm, up_b_hbm,
     out_hbm, state_hbm, first_hbm, second_hbm,
-    x_buf, partial, sums, turned, own_stat, peer_stat, rest, give, got, parcel, arrived, stat_out, stat_in,
+    x_buf, partial, sums, turned, own_stat, peer_stat, rest, give, got, across, crossed, parcel, arrived, stat_out, stat_in,
     sent, beside, conv_w, up_w, first_w, second_w, previous, taps, wide, stage, ready, state,
     shift_ref, scale_ref, head_w_ref, head_b_ref, lat_mean_ref, lat_std_ref, conv_b_ref, up_b_ref,
     x_sem, w_sem, stat_sem, core_send, core_recv, send_sem, recv_sem, ssend_sem, srecv_sem, hsend_sem, hrecv_sem,
-    out_sem, keep_sem, small_sem,
+    out_sem, keep_sem, small_sem, y_sem,
 ):
     me = lax.axis_index("sp")
     req = lax.axis_index("req")
@@ -224,15 +226,32 @@
             parcel.at[c, k], arrived.at[c, k], send_sem.at[c, k], recv_sem.at[c, k], (req, chips[k] * 2 + core)
         )
 
-    def dispatch(c):
+    def merged(c, k):
+        return gathered(c, chips[k], core) + got[c, k].astype(F32)
+
+    def across_copy(c):
+        return remote(
+            across.at[c], crossed.at[c], y_sem.at[c, 0], y_sem.at[c, 1], (req, chips[CHIPS - 2] * 2 + core)
+        )
+
+    def dispatch_across(c):
         core_copy(c).wait_recv()
-        for k in range(CHIPS):
-            merged = gathered(c, chips[k], core) + got[c, k].astype(F32)
-            if k == CHIPS - 1:
-                rest[c] = merged
-            else:
-                parcel[c, k] = merged.astype(BF16)
-                parcel_copy(c, k).start()
+        for i in range(FAR // 2):
+            across[c, i] = merged(c, 2 * i).astype(BF16)
+        across_copy(c).start()
+
+    def dispatch_near(c):
+        for k in range(FAR, CHIPS - 1):
+            parcel[c, k] = merged(c, k).astype(BF16)
+            parcel_copy(c, k).start()
+        rest[c] = merged(c, CHIPS - 1)
+
+    def dispatch_far(c):
+        across_copy(c).wait_recv()
+        for i in range(FAR // 2):
+            k = 2 * i + 1
+            parcel[c, k] = (merged(c, k) + crossed[c, i].astype(F32)).astype(BF16)
+            parcel_copy(c, k).start()
 
     for c in range(CHUNKS):
         x_copies[c].wait()
@@ -275,7 +294,9 @@
     own_stat[4] = jnp.broadcast_to(own_row, (32, 128))
     stat_copy = remote(own_stat, peer_stat, stat_sem.at[0], stat_sem.at[1], partner)
     stat_copy.start()
-    dispatch(0)
+    for c in range(CHUNKS):
+        dispatch_across(c)
+    dispatch_near(0)
     stat_copy.wait()
 
     low_half = lanes((32, 128)) < 64
@@ -304,8 +325,7 @@
             stat_out[k] = value
             stat_remote(k).start()
 
-    dispatch(1)
-    dispatch(2)
+    dispatch_near(1)
     conv_copy.wait()
     prepare_first(conv_w, first_w)
     up_copy.wait()
@@ -318,6 +338,10 @@
     for copy in keeps:
         copy.start()
 
+    dispatch_far(0)
+    dispatch_near(2)
+    dispatch_far(1)
+    dispatch_far(2)
     for k in range(CHIPS - 1):
         stat_remote(k).wait_recv()
     total = jnp.sum(stat_in[...].reshape(CHIPS, 8, 128), axis=0)
@@ -357,10 +381,10 @@
         pl.when(me < GROUP - 1)(getattr(to_right, action))
 
     def finish(c):
-        for k in range(CHIPS - 1):
+        for k in SLOTS:
             parcel_copy(c, k).wait_recv()
         value = rest[c]
-        for k in range(CHIPS - 1):
+        for k in SLOTS:
             value = value + arrived[c, k].astype(F32)
         none = jnp.zeros((8, 128), F32)
         spread = []
@@ -390,7 +414,8 @@
         out_copy(c).start()
 
     finish(0)
-    dispatch(3)
+    dispatch_near(3)
+    dispatch_far(3)
     finish(1)
     decode(0)
     finish(2)
@@ -410,7 +435,8 @@
         if c < CHUNKS - 1:
             out_copy(c).wait()
         core_copy(c).wait_send()
-        for k in range(CHIPS - 1):
+        across_copy(c).wait_send()
+        for k in SLOTS:
             parcel_copy(c, k).wait_send()
         ends(c, "wait_send")
     for k in range(CHIPS - 1):
@@ -484,6 +510,8 @@
             pltpu.VMEM((CHUNKS, 32, 128), F32),
             pltpu.VMEM((CHUNKS, CHIPS, 32, 128), BF16),
             pltpu.VMEM((CHUNKS, CHIPS, 32, 128), BF16),
+            pltpu.VMEM((CHUNKS, FAR // 2, 32, 128), BF16),
+            pltpu.VMEM((CHUNKS, FAR // 2, 32, 128), BF16),
             pltpu.VMEM((CHUNKS, CHIPS, 32, 128), BF16),
             pltpu.VMEM((CHUNKS, CHIPS, 32, 128), BF16),
             pltpu.VMEM((CHIPS, 8, 128), F32),
@@ -519,6 +547,7 @@
             dma((CHUNKS,)),
             dma((3,)),
             dma((8,)),
+            dma((CHUNKS, 2)),
         ],
         compiler_params=pltpu.CompilerParams(
             collective_id=0, has_side_effects=True, vmem_limit_bytes=62 * 1024 * 1024

time: 39.2 us -> 38.1 us (0.972)
  the two profiles are of different devices: /device:TPU:1 before, /device:TPU:28 now
where the time goes in v4:
time: 38.1 us; the launch traced here: 38 us
  Pallas kernels  38 us (100%)
    pallas_call x1, Pallas kernels, shards(): pl.pallas_call(reduce_kernel, out_shape=[jax.ShapeDtypeStruct((6, 8, 2, 4...  33.4 us
    pallas_call x1, Pallas kernels, shards(): pl.pallas_call(last_kernel, out_shape=pieces, in_specs=[hbm] * 4, out_spe...  4.58 us

profile of v4, /device:TPU:28, one launch (start us, length us, event | category | flops | bytes accessed | tf_op | source)
XLA Modules:
  0.0 38.0 jit_solution(3878021420152849482)
XLA Ops:
  0.0 33.4 %reduce.1 = (bf16[6,8,2,4,8,192]{5,4,3,2,1,0:T(8,128)(2,1)}, f32[4,64,128]{2,1,0:T(8,128)}, bf16[3,256,768]{2,1,0:T(8,128)(2,1)}, bf16[2,2,2,256,768]{4,3,2,1,0:T(8,128)(2,1)}) custom-call(bf16[160,8192]{1,0:T(8,128)(2,1)} %bitcast.4, f32[160]{0:T(256)} %shift_hbm.1, f32[160]{0:T(256)} %scale_hbm.1, bf16[64,160]{1,0:T(8,128)(2,1)} %bitcast.6, f32[64]{0:T(128)} %head_b_hbm.1, ...), custom_call_target="tpu_custom_call" | custom-call | tf_op jit(solution)/shard_map/reduce/pallas_call | solution.py:498
  33.4 4.6 %last.1 = bf16[8,8,2,4,8,192]{5,4,3,2,1,0:T(8,128)(2,1)} custom-call(bf16[6,8,2,4,8,192]{5,4,3,2,1,0:T(8,128)(2,1)} %get-tuple-element.9.done_hbm, f32[4,64,128]{2,1,0:T(8,128)} %get-tuple-element.10.state_hbm, bf16[3,256,768]{2,1,0:T(8,128)(2,1)} %get-tuple-element.11.first_hbm, bf16[2,2,2,256,768]{4,3,2,1,0:T(8,128)(2,1)} %get-tuple-element.12.second_hbm), custom_call_target="tpu_custom_call" | custom-call | tf_op jit(solution)/shard_map/last/pallas_call | solution.py:560

commit v5 on v4

--- a/solution.py
+++ b/solution.py
@@ -344,7 +344,7 @@
     dispatch_far(2)
     for k in range(CHIPS - 1):
         stat_remote(k).wait_recv()
-    total = jnp.sum(stat_in[...].reshape(CHIPS, 8, 128), axis=0)
+    total = jnp.sum(stat_in[0 : CHIPS * 8, :].reshape(CHIPS, 8, 128), axis=0)
     sums_of = [stat_in[pl.ds(c, CHIPS, stride=8), :] for c in range(4)]
     heads = stat_in[pl.ds(6, CHIPS, stride=8), :]
     heads = jnp.concatenate([heads, pltpu.roll(heads, 64, 1), jnp.zeros((96, 128), F32)], axis=0)
@@ -488,7 +488,7 @@
         pltpu.VMEM((2, 64, 128), F32),
         pltpu.VMEM((256, 256), BF16),
         pltpu.VMEM((2, 192, 1152), BF16),
-        pltpu.VMEM((2, 1024, 128), F32),
+        pltpu.VMEM((2, 1032, 128), F32),
     ]
     held = [
         jax.ShapeDtypeStruct((4, 64, 128), F32),
@@ -502,9 +502,9 @@
         out_specs=[hbm] * 4,
         scratch_shapes=[
             pltpu.VMEM((CHUNKS, LOCAL, 2048), BF16),
-            pltpu.VMEM((CHUNKS, 1024, 128), F32),
+            pltpu.VMEM((CHUNKS, 1152, 128), F32),
             pltpu.VMEM((128, 128), F32),
-            pltpu.VMEM((256, 128), F32),
+            pltpu.VMEM((264, 128), F32),
             pltpu.VMEM((5, 32, 128), F32),
             pltpu.VMEM((5, 32, 128), F32),
             pltpu.VMEM((CHUNKS, 32, 128), F32),
@@ -515,7 +515,7 @@
             pltpu.VMEM((CHUNKS, CHIPS, 32, 128), BF16),
             pltpu.VMEM((CHUNKS, CHIPS, 32, 128), BF16),
             pltpu.VMEM((CHIPS, 8, 128), F32),
-            pltpu.VMEM((CHIPS * 8, 128), F32),
+            pltpu.VMEM((CHIPS * 8 + 8, 128), F32),
             pltpu.VMEM((CHUNKS, 64, 128), BF16),
             pltpu.VMEM((CHUNKS, 2, 64, 128), BF16),
             pltpu.VMEM((3, 3, 3, 16, 384), BF16),

time: 38.1 us -> 38.1 us (level)
  the two profiles are of different devices: /device:TPU:28 before, /device:TPU:18 now
where the time goes in v5:
time: 38.1 us; the launch traced here: 38 us
  Pallas kernels  38 us (100%)
    pallas_call x1, Pallas kernels, shards(): pl.pallas_call(reduce_kernel, out_shape=[jax.ShapeDtypeStruct((6, 8, 2, 4...  33.4 us
    pallas_call x1, Pallas kernels, shards(): pl.pallas_call(last_kernel, out_shape=pieces, in_specs=[hbm] * 4, out_spe...  4.59 us

profile of v5, /device:TPU:18, one launch (start us, length us, event | category | flops | bytes accessed | tf_op | source)
XLA Modules:
  0.0 38.0 jit_solution(9124245222839116479)
XLA Ops:
  0.0 33.4 %reduce.1 = (bf16[6,8,2,4,8,192]{5,4,3,2,1,0:T(8,128)(2,1)}, f32[4,64,128]{2,1,0:T(8,128)}, bf16[3,256,768]{2,1,0:T(8,128)(2,1)}, bf16[2,2,2,256,768]{4,3,2,1,0:T(8,128)(2,1)}) custom-call(bf16[160,8192]{1,0:T(8,128)(2,1)} %bitcast.4, f32[160]{0:T(256)} %shift_hbm.1, f32[160]{0:T(256)} %scale_hbm.1, bf16[64,160]{1,0:T(8,128)(2,1)} %bitcast.6, f32[64]{0:T(128)} %head_b_hbm.1, ...), custom_call_target="tpu_custom_call" | custom-call | tf_op jit(solution)/shard_map/reduce/pallas_call | solution.py:498
  33.4 4.6 %last.1 = bf16[8,8,2,4,8,192]{5,4,3,2,1,0:T(8,128)(2,1)} custom-call(bf16[6,8,2,4,8,192]{5,4,3,2,1,0:T(8,128)(2,1)} %get-tuple-element.9.done_hbm, f32[4,64,128]{2,1,0:T(8,128)} %get-tuple-element.10.state_hbm, bf16[3,256,768]{2,1,0:T(8,128)(2,1)} %get-tuple-element.11.first_hbm, bf16[2,2,2,256,768]{4,3,2,1,0:T(8,128)(2,1)} %get-tuple-element.12.second_hbm), custom_call_target="tpu_custom_call" | custom-call | tf_op jit(solution)/shard_map/last/pallas_call | solution.py:560
